TPU v7x, 256 devices: a whole 4x4x8 slice. The times are simulated.
256 devices in a mesh: dp: 32 (over y, z), tensor: 8 (over x, core).
Axes of the slice: x: 4, y: 4, z: 8, core: 2. Of those that a mesh axis runs over, the one named last changes fastest.
Arguments:
- queries: bfloat16 [16384, 8192], P('dp', 'tensor'), may hold values from -140 to 140
- keys: bfloat16 [16384, 1024], P('dp', 'tensor'), may hold values from -6 to 6
- values: bfloat16 [16384, 1024], P('dp', 'tensor'), may hold values from -6 to 6
- out_grad: bfloat16 [16384, 3072], P('dp', 'tensor'), may hold values from -6 to 6
- out_weight: bfloat16 [8192, 3072], P('tensor'), may hold values from -0.109375 to 0.109375
- send_slot: int32 [16384], P('dp'), may hold values from 0 to 1023, as said below
- recv_index: int32 [16384], P('dp'), may hold values from 0 to 1023, as said below
- packed_doc: int32 [16384], P('dp'), may hold values from 0 to 127, as said below
Outputs:
- query_grad: bfloat16 [16384, 8192], P('dp', 'tensor')
- key_grad: bfloat16 [16384, 1024], P('dp', 'tensor')
- value_grad: bfloat16 [16384, 1024], P('dp', 'tensor')
- weight_grad: float32 [3072, 8192], P('dp', 'tensor')
Inputs may be any that keep to these rules, and one draw needn't show every extreme that they name: `send_slot`: for the 512 tokens of one index of dp the values are distinct; a value s sends the token to index s // 32 of dp, into place s % 32 among the tokens sent there. The places used from one index toward one index are 0, 1, ... without gaps, at most 32 of them, and every index receives exactly 512 tokens. `recv_index`: on each index of dp the 512 values are distinct and name exactly the received places that were filled, as source * 32 + place, sources increasing and places increasing within a source; entry i gives packed row i. `packed_doc`: on each index of dp the document number starts at 0 and rises by 0 or 1 from one packed row to the next.
All inputs are finite; a program needn't handle non-finite values.
Results may differ from a plain program's by a relative error of at most 0.02.
Values may be sent and summed in bfloat16 or wider, within the bound.
A program may use at most 128 MiB of HBM per device.

v0:
```python
import math

import jax
import jax.numpy as jnp
from jax import lax
from jax.sharding import PartitionSpec as P

HEADS = 64
KV_HEADS = 8
HEAD_DIM = 128


def spread(block, slots, lanes):
    holder = jnp.zeros((lanes,) + block.shape[1:], block.dtype)
    return holder.at[slots].set(block)


def attention_backward(query_pack, key_pack, value_pack, head_grad, doc_rank):
    tok_rows = query_pack.shape[0]
    kv_local = key_pack.shape[1] // HEAD_DIM
    group = HEADS // KV_HEADS
    inv_root = 1.0 / math.sqrt(HEAD_DIM)
    query_heads = query_pack.reshape(tok_rows, kv_local, group, HEAD_DIM)
    key_heads = key_pack.reshape(tok_rows, kv_local, HEAD_DIM)
    value_heads = value_pack.reshape(tok_rows, kv_local, HEAD_DIM)
    grad_heads = head_grad.reshape(tok_rows, kv_local, group, HEAD_DIM)
    scores = (
        jnp.einsum("tkgd,skd->kgts", query_heads, key_heads, preferred_element_type=jnp.float32)
        * inv_root
    )
    places = jnp.arange(tok_rows, dtype=jnp.int32)
    visible = (doc_rank[:, None] == doc_rank[None, :]) & (places[None, :] <= places[:, None])
    scores = jnp.where(visible, scores, -1e30)
    row_top = jnp.max(scores, axis=-1, keepdims=True)
    raised = jnp.exp(scores - row_top)
    soft = raised / jnp.sum(raised, axis=-1, keepdims=True)
    soft_half = soft.astype(jnp.bfloat16)
    attended = jnp.einsum(
        "kgts,skd->tkgd", soft_half, value_heads, preferred_element_type=jnp.float32
    )
    attended = attended.astype(jnp.bfloat16).reshape(tok_rows, -1)
    soft_grad = jnp.einsum(
        "tkgd,skd->kgts", grad_heads, value_heads, preferred_element_type=jnp.float32
    )
    inner = jnp.sum(soft * soft_grad, axis=-1, keepdims=True)
    score_grad = (soft * (soft_grad - inner)).astype(jnp.bfloat16)
    query_delta = (
        jnp.einsum("kgts,skd->tkgd", score_grad, key_heads, preferred_element_type=jnp.float32)
        * inv_root
    ).astype(jnp.bfloat16)
    key_delta = (
        jnp.einsum("kgts,tkgd->skd", score_grad, query_heads, preferred_element_type=jnp.float32)
        * inv_root
    ).astype(jnp.bfloat16)
    value_delta = jnp.einsum(
        "kgts,tkgd->skd", soft_half, grad_heads, preferred_element_type=jnp.float32
    ).astype(jnp.bfloat16)
    return (
        attended,
        query_delta.reshape(tok_rows, -1),
        key_delta.reshape(tok_rows, -1),
        value_delta.reshape(tok_rows, -1),
    )


def shards(queries, keys, values, out_grad, out_weight, send_slot, recv_index, packed_doc):
    tok_rows = queries.shape[0]
    peers = lax.axis_size("dp")
    lanes = 2 * tok_rows
    grad_slab = lax.all_gather(out_grad, "tensor", axis=1, tiled=True)
    moved = (
        lax.all_to_all(
            spread(queries, send_slot, lanes), "dp", split_axis=0, concat_axis=0, tiled=True
        ),
        lax.all_to_all(
            spread(keys, send_slot, lanes), "dp", split_axis=0, concat_axis=0, tiled=True
        ),
        lax.all_to_all(
            spread(values, send_slot, lanes), "dp", split_axis=0, concat_axis=0, tiled=True
        ),
        lax.all_to_all(
            spread(grad_slab, send_slot, lanes), "dp", split_axis=0, concat_axis=0, tiled=True
        ),
    )
    query_pack = moved[0][recv_index]
    key_pack = moved[1][recv_index]
    value_pack = moved[2][recv_index]
    grad_full = moved[3][recv_index]
    head_grad = lax.dot_general(
        grad_full, out_weight, (((1,), (1,)), ((), ())), preferred_element_type=jnp.float32
    ).astype(jnp.bfloat16)
    attended, query_delta, key_delta, value_delta = attention_backward(
        query_pack, key_pack, value_pack, head_grad, packed_doc
    )
    norm_scale = 1.0 / math.sqrt(tok_rows * peers)
    weight_grad = lax.psum_scatter(
        (
            lax.dot_general(
                grad_full, attended, (((0,), (0,)), ((), ())), preferred_element_type=jnp.float32
            )
            * norm_scale
        ).astype(jnp.bfloat16),
        "dp",
        scatter_dimension=0,
        tiled=True,
    ).astype(jnp.float32)
    returned = (
        lax.all_to_all(
            spread(query_delta, recv_index, lanes), "dp", split_axis=0, concat_axis=0, tiled=True
        ),
        lax.all_to_all(
            spread(key_delta, recv_index, lanes), "dp", split_axis=0, concat_axis=0, tiled=True
        ),
        lax.all_to_all(
            spread(value_delta, recv_index, lanes), "dp", split_axis=0, concat_axis=0, tiled=True
        ),
    )
    return (returned[0][send_slot], returned[1][send_slot], returned[2][send_slot], weight_grad)


def solution(mesh):
    placed = (
        P("dp", "tensor"),
        P("dp", "tensor"),
        P("dp", "tensor"),
        P("dp", "tensor"),
        P("tensor", None),
        P("dp"),
        P("dp"),
        P("dp"),
    )
    return jax.shard_map(
        shards,
        mesh=mesh,
        in_specs=placed,
        out_specs=(P("dp", "tensor"), P("dp", "tensor"), P("dp", "tensor"), P("dp", "tensor")),
        check_vma=False,
    )
```

profile of v0, /device:TPU:4, one launch (start us, length us, event | category | flops | bytes accessed | tf_op | source)
XLA Modules:
  0.0 536.1 jit_solution(9370978017595275405)
XLA Ops:
  8.6 2.8 scatter_custom_fusion
  11.4 11.5 %all-to-all-start = ((bf16[32,32,128]{2,1,0:T(8,128)(2,1)}), bf16[32,32,128]{2,1,0:T(8,128)(2,1)S(1)}, u32[]{:S(2)}, u32[]{:S(2)}) async-start(bf16[32,32,128]{2,1,0:T(8,128)(2,1)} %bitcast), calls=%async_computation | async-start | bytes 524288 | tf_op jit(solution)/shard_map/all_to_all | solution.py:75
  22.9 2.8 scatter_custom_fusion.2
  25.6 9.7 %all-to-all-done = bf16[32,32,128]{2,1,0:T(8,128)(2,1)S(1)} async-done(((bf16[32,32,128]{2,1,0:T(8,128)(2,1)}), bf16[32,32,128]{2,1,0:T(8,128)(2,1)S(1)}, u32[]{:S(2)}, u32[]{:S(2)}) %all-to-all-start) | async-done | bytes 262176 | tf_op jit(solution)/shard_map/all_to_all | solution.py:75
  35.3 4.4 all-to-all-start.2
  39.7 4.8 scatter_custom_fusion.1
  44.5 6.6 %all-to-all-done.2 = bf16[32,32,128]{2,1,0:T(8,128)(2,1)S(1)} async-done(((bf16[32,32,128]{2,1,0:T(8,128)(2,1)}), bf16[32,32,128]{2,1,0:T(8,128)(2,1)S(1)}, u32[]{:S(2)}, u32[]{:S(2)}) %all-to-all-start.2) | async-done | bytes 262176 | tf_op jit(solution)/shard_map/all_to_all | solution.py:78
  51.1 5.1 all-to-all-start.1
  56.3 9.9 %scatter_custom_fusion.3 = bf16[1024,3072]{1,0:T(8,128)(2,1)} fusion(s32[512]{0:T(512)S(1)} %compare_select_fusion, bf16[512,3072]{1,0:T(8,128)(2,1)} %all-gather.2.cloned.1.call-done, bf16[]{:T(256)} %constant.8.clone.1), kind=kCustom, calls=%fused_computation.27 | custom fusion | bytes 6291968 | tf_op jit(solution)/shard_map/scatter | solution.py:15
  66.1 39.0 %all-to-all-done.1 = bf16[32,32,1024]{2,1,0:T(8,128)(2,1)S(1)} async-done(((bf16[32,32,1024]{2,1,0:T(8,128)(2,1)}), bf16[32,32,1024]{2,1,0:T(8,128)(2,1)S(1)}, u32[]{:S(2)}, u32[]{:S(2)}) %all-to-all-start.1) | async-done | bytes 2097184 | tf_op jit(solution)/shard_map/all_to_all | solution.py:72
  105.2 6.0 %all-to-all-start.3 = ((bf16[32,32,3072]{2,1,0:T(8,128)(2,1)}), bf16[32,32,3072]{2,1,0:T(8,128)(2,1)}, u32[]{:S(2)}, u32[]{:S(2)}) async-start(bf16[32,32,3072]{2,1,0:T(8,128)(2,1)} %bitcast.133), calls=%async_computation.3 | async-start | bytes 12582912 | tf_op jit(solution)/shard_map/all_to_all | solution.py:81
  118.8 3.3 copy-done
  123.9 125.1 %all-to-all-done.3 = bf16[32,32,3072]{2,1,0:T(8,128)(2,1)} async-done(((bf16[32,32,3072]{2,1,0:T(8,128)(2,1)}), bf16[32,32,3072]{2,1,0:T(8,128)(2,1)}, u32[]{:S(2)}, u32[]{:S(2)}) %all-to-all-start.3) | async-done | bytes 6291488 | tf_op jit(solution)/shard_map/all_to_all | solution.py:81
  249.0 10.6 %gather_fusion.3 = bf16[512,3072]{1,0:T(8,128)(2,1)} fusion(bf16[1024,3072]{1,0:T(8,128)(2,1)} %bitcast.12, s32[1024]{0:T(1024)S(1)} %pad_clamp_fusion.1), kind=kCustom, calls=%fused_computation.3 | custom fusion | bytes 6293504 | tf_op jit(solution)/shard_map/gather | solution.py:88
  259.6 7.3 %convolution_convert_fusion.1 = bf16[512,1024]{1,0:T(8,128)(2,1)S(1)} fusion(bf16[512,3072]{1,0:T(8,128)(2,1)} %gather_fusion.3, bf16[1024,3072]{1,0:T(8,128)(2,1)} %param.12), kind=kOutput, calls=%fused_computation.31 | convolution fusion | flops 3221749760 | bytes 10485760 | tf_op jit(solution)/shard_map/dot_general | solution.py:89
  267.0 3.2 fusion
  270.2 4.4 convert_bitcast_fusion
  277.4 5.5 %multiply_convert_fusion = bf16[3072,1024]{1,0:T(8,128)(2,1)} fusion(bf16[512,3072]{1,0:T(8,128)(2,1)S(1)} %copy-done.3, bf16[512,1024]{0,1:T(8,128)(2,1)S(1)} %bitcast.145), kind=kOutput, calls=%fused_computation.14 | convolution fusion | flops 3227516928 | bytes 10485760 | tf_op jit(solution)/shard_map/dot_general | solution.py:98
  282.9 8.1 %copy.40 = bf16[8,512,512]{2,0,1:T(8,128)(2,1)} copy(bf16[8,512,512]{1,2,0:T(8,128)(2,1)} %copy-done.2) | data formatting | bytes 8388608 | tf_op jit(solution)/shard_map/reshape.28
  291.3 3.0 fusion.12
  296.8 8.0 %all-to-all-start.6 = ((bf16[32,32,128]{2,1,0:T(8,128)(2,1)}), bf16[32,32,128]{2,1,0:T(8,128)(2,1)S(1)}, u32[]{:S(2)}, u32[]{:S(2)}) async-start(bf16[32,32,128]{2,1,0:T(8,128)(2,1)} %bitcast.33), calls=%async_computation.6 | async-start | bytes 524288 | tf_op jit(solution)/shard_map/all_to_all | solution.py:114
  305.2 8.1 %copy.38 = bf16[8,512,512]{2,0,1:T(8,128)(2,1)} copy(bf16[8,512,512]{1,2,0:T(8,128)(2,1)} %get-tuple-element.5) | data formatting | bytes 8388608 | tf_op jit(solution)/shard_map/reshape.18
  313.2 3.0 fusion.13
  316.4 2.4 scatter_custom_fusion.5
  318.8 10.0 %all-to-all-start.5 = ((bf16[32,32,128]{2,1,0:T(8,128)(2,1)}), bf16[32,32,128]{2,1,0:T(8,128)(2,1)S(1)}, u32[]{:S(2)}, u32[]{:S(2)}) async-start(bf16[32,32,128]{2,1,0:T(8,128)(2,1)} %bitcast.26), calls=%async_computation.5 | async-start | bytes 524288 | tf_op jit(solution)/shard_map/all_to_all | solution.py:111
  328.8 2.9 multiply_convert_fusion.1
  332.3 4.2 scatter_custom_fusion.4
  336.5 5.1 all-to-all-done.5
  341.6 5.0 all-to-all-start.4
  350.4 58.9 %all-to-all-done.4 = bf16[32,32,1024]{2,1,0:T(8,128)(2,1)S(1)} async-done(((bf16[32,32,1024]{2,1,0:T(8,128)(2,1)}), bf16[32,32,1024]{2,1,0:T(8,128)(2,1)S(1)}, u32[]{:S(2)}, u32[]{:S(2)}) %all-to-all-start.4) | async-done | bytes 2097184 | tf_op jit(solution)/shard_map/all_to_all | solution.py:108
  409.3 2.8 gather_fusion.4
  412.1 115.1 %reduce-scatter.2.cloned.1.call-done = bf16[96,1024]{1,0:T(8,128)(2,1)} async-done(((bf16[3072,1024]{1,0:T(8,128)(2,1)}), bf16[96,1024]{1,0:T(8,128)(2,1)}) %reduce-scatter.2.cloned.1.call-update) | async-done | bytes 196624 | tf_op jit(solution)/shard_map/reduce_scatter | solution.py:96
  (43 shorter events, 22.9 us)
Async XLA Ops:
  7.2 49.1 %all-gather.2.cloned.1.call-start = ((), (), s32[]{:S(2)}) async-start(), calls=%async_computation.8 | async-start | bytes 3538944 | tf_op jit(solution)/shard_map/all_gather | solution.py:70
  11.4 23.9 %all-to-all-start = ((bf16[32,32,128]{2,1,0:T(8,128)(2,1)}), bf16[32,32,128]{2,1,0:T(8,128)(2,1)S(1)}, u32[]{:S(2)}, u32[]{:S(2)}) async-start(bf16[32,32,128]{2,1,0:T(8,128)(2,1)} %bitcast), calls=%async_computation | async-start | bytes 524288 | tf_op jit(solution)/shard_map/all_to_all | solution.py:75
  35.3 15.8 %all-to-all-start.2 = ((bf16[32,32,128]{2,1,0:T(8,128)(2,1)}), bf16[32,32,128]{2,1,0:T(8,128)(2,1)S(1)}, u32[]{:S(2)}, u32[]{:S(2)}) async-start(bf16[32,32,128]{2,1,0:T(8,128)(2,1)} %bitcast.8), calls=%async_computation.2 | async-start | bytes 524288 | tf_op jit(solution)/shard_map/all_to_all | solution.py:78
  51.1 54.0 %all-to-all-start.1 = ((bf16[32,32,1024]{2,1,0:T(8,128)(2,1)}), bf16[32,32,1024]{2,1,0:T(8,128)(2,1)S(1)}, u32[]{:S(2)}, u32[]{:S(2)}) async-start(bf16[32,32,1024]{2,1,0:T(8,128)(2,1)} %bitcast.136), calls=%async_computation.1 | async-start | bytes 4194304 | tf_op jit(solution)/shard_map/all_to_all | solution.py:72
  105.2 6.2 %copy-start.8 = (s32[512]{0:T(512)S(1)}, s32[512]{0:T(512)}, u32[]{:S(2)}) copy-start(s32[512]{0:T(512)} %param.14) | copy-start | bytes 6148
  105.2 6.2 %copy-start.7 = (s32[512]{0:T(512)S(1)}, s32[512]{0:T(512)}, u32[]{:S(2)}) copy-start(s32[512]{0:T(512)} %param.15) | copy-start | bytes 6148
  105.2 143.8 %all-to-all-start.3 = ((bf16[32,32,3072]{2,1,0:T(8,128)(2,1)}), bf16[32,32,3072]{2,1,0:T(8,128)(2,1)}, u32[]{:S(2)}, u32[]{:S(2)}) async-start(bf16[32,32,3072]{2,1,0:T(8,128)(2,1)} %bitcast.133), calls=%async_computation.3 | async-start | bytes 12582912 | tf_op jit(solution)/shard_map/all_to_all | solution.py:81
  111.1 416.0 %reduce-scatter.2.cloned.1.call-start = ((), (), s32[]{:S(2)}) async-start(), calls=%async_computation.9 | async-start | bytes 6488064 | tf_op jit(solution)/shard_map/reduce_scatter | solution.py:96
  118.8 3.3 copy-start
  259.6 7.3 %copy-start.1 = (f32[512,512,8]{1,0,2:T(8,128)S(1)}, f32[512,512,8]{1,0,2:T(8,128)}, u32[]{:S(2)}) copy-start(f32[512,512,8]{1,0,2:T(8,128)} %copy-done) | copy-start | bytes 25165828
  259.6 7.3 %copy-start.6 = (bf16[512,128]{1,0:T(8,128)(2,1)S(1)}, bf16[512,128]{1,0:T(8,128)(2,1)}, u32[]{:S(2)}) copy-start(bf16[512,128]{1,0:T(8,128)(2,1)} %gather_fusion.2) | copy-start | bytes 393220
  267.0 3.2 copy-start.4
  270.2 7.2 %copy-start.3 = (bf16[512,3072]{1,0:T(8,128)(2,1)S(1)}, bf16[512,3072]{1,0:T(8,128)(2,1)}, u32[]{:S(2)}) copy-start(bf16[512,3072]{1,0:T(8,128)(2,1)} %gather_fusion.3) | copy-start | bytes 9437188
  274.6 2.1 copy-start.2
  282.9 8.1 %copy-start.5 = (bf16[512,1024]{1,0:T(8,128)(2,1)S(1)}, bf16[512,1024]{1,0:T(8,128)(2,1)}, u32[]{:S(2)}) copy-start(bf16[512,1024]{1,0:T(8,128)(2,1)} %copy-done.4) | copy-start | bytes 3145732
  296.8 21.9 %all-to-all-start.6 = ((bf16[32,32,128]{2,1,0:T(8,128)(2,1)}), bf16[32,32,128]{2,1,0:T(8,128)(2,1)S(1)}, u32[]{:S(2)}, u32[]{:S(2)}) async-start(bf16[32,32,128]{2,1,0:T(8,128)(2,1)} %bitcast.33), calls=%async_computation.6 | async-start | bytes 524288 | tf_op jit(solution)/shard_map/all_to_all | solution.py:114
  318.8 22.8 %all-to-all-start.5 = ((bf16[32,32,128]{2,1,0:T(8,128)(2,1)}), bf16[32,32,128]{2,1,0:T(8,128)(2,1)S(1)}, u32[]{:S(2)}, u32[]{:S(2)}) async-start(bf16[32,32,128]{2,1,0:T(8,128)(2,1)} %bitcast.26), calls=%async_computation.5 | async-start | bytes 524288 | tf_op jit(solution)/shard_map/all_to_all | solution.py:111
  341.6 67.8 %all-to-all-start.4 = ((bf16[32,32,1024]{2,1,0:T(8,128)(2,1)}), bf16[32,32,1024]{2,1,0:T(8,128)(2,1)S(1)}, u32[]{:S(2)}, u32[]{:S(2)}) async-start(bf16[32,32,1024]{2,1,0:T(8,128)(2,1)} %bitcast.135), calls=%async_computation.4 | async-start | bytes 4194304 | tf_op jit(solution)/shard_map/all_to_all | solution.py:108
Sparse Core Ops, SparseCore 0:
  9.8 31.8 all-gather.1
  283.0 244.0 reduce-scatter.1
where the time goes:
time: 543 us; the launch traced here: 536 us
  waiting for transfers between devices  360 us (66%)
  local copies, waits for them, and re-layouts  74.7 us (14%)
  starting transfers between devices  50.2 us (9%)
  matrix products  27.5 us (5%)
  between operations  14.8 us (3%)
  other arithmetic  8.74 us (2%)
    all_to_all x1, waiting for transfers between devices, shards(): lax.all_to_all(spread(grad_slab, send_slot, lanes), 'dp', split_axis=0, c...  125 us
    reduce_scatter x1, waiting for transfers between devices, shards(): lax.psum_scatter((lax.dot_general(grad_full, attended, (((0,), (0,)), (()...  115 us
    all_to_all x1, waiting for transfers between devices, shards(): lax.all_to_all(spread(query_delta, recv_index, lanes), 'dp', split_axis=0...  58.9 us
    all_to_all x1, waiting for transfers between devices, shards(): lax.all_to_all(spread(queries, send_slot, lanes), 'dp', split_axis=0, con...  39 us
    scatter x7, local copies, waits for them, and re-layouts, spread(): return holder.at[slots].set(block)  29.3 us
    another operation x2, local copies, waits for them, and re-layouts  16.2 us
    all_to_all x1, starting transfers between devices, shards(): lax.all_to_all(spread(keys, send_slot, lanes), 'dp', split_axis=0, concat...  11.5 us
  transfers between devices with their start and end apart: 9, of which 7 were waited for; matrix products, arithmetic and copies ran while one was open for 13% of the time, Pallas kernels for 0%

commit v1 on v0

v1 whole, which is shorter than its diff:
```python
import functools
import math

import jax
import jax.numpy as jnp
from jax import lax
from jax.experimental import pallas as pl
from jax.experimental.pallas import tpu as pltpu
from jax.sharding import PartitionSpec as P

HEADS = 64
KV_HEADS = 8
HEAD_DIM = 128
MESH = pl.DeviceIdType.MESH


def attention_backward(query_pack, key_pack, value_pack, head_grad, doc_rank):
    tok_rows = query_pack.shape[0]
    kv_local = key_pack.shape[1] // HEAD_DIM
    group = HEADS // KV_HEADS
    inv_root = 1.0 / math.sqrt(HEAD_DIM)
    query_heads = query_pack.reshape(tok_rows, kv_local, group, HEAD_DIM)
    key_heads = key_pack.reshape(tok_rows, kv_local, HEAD_DIM)
    value_heads = value_pack.reshape(tok_rows, kv_local, HEAD_DIM)
    grad_heads = head_grad.reshape(tok_rows, kv_local, group, HEAD_DIM)
    scores = (
        jnp.einsum("tkgd,skd->kgts", query_heads, key_heads, preferred_element_type=jnp.float32)
        * inv_root
    )
    places = jnp.arange(tok_rows, dtype=jnp.int32)
    visible = (doc_rank[:, None] == doc_rank[None, :]) & (places[None, :] <= places[:, None])
    scores = jnp.where(visible, scores, -1e30)
    row_top = jnp.max(scores, axis=-1, keepdims=True)
    raised = jnp.exp(scores - row_top)
    soft = raised / jnp.sum(raised, axis=-1, keepdims=True)
    soft_half = soft.astype(jnp.bfloat16)
    attended = jnp.einsum(
        "kgts,skd->tkgd", soft_half, value_heads, preferred_element_type=jnp.float32
    )
    attended = attended.astype(jnp.bfloat16).reshape(tok_rows, -1)
    soft_grad = jnp.einsum(
        "tkgd,skd->kgts", grad_heads, value_heads, preferred_element_type=jnp.float32
    )
    inner = jnp.sum(soft * soft_grad, axis=-1, keepdims=True)
    score_grad = (soft * (soft_grad - inner)).astype(jnp.bfloat16)
    query_delta = (
        jnp.einsum("kgts,skd->tkgd", score_grad, key_heads, preferred_element_type=jnp.float32)
        * inv_root
    ).astype(jnp.bfloat16)
    key_delta = (
        jnp.einsum("kgts,tkgd->skd", score_grad, query_heads, preferred_element_type=jnp.float32)
        * inv_root
    ).astype(jnp.bfloat16)
    value_delta = jnp.einsum(
        "kgts,tkgd->skd", soft_half, grad_heads, preferred_element_type=jnp.float32
    ).astype(jnp.bfloat16)
    return (
        attended,
        query_delta.reshape(tok_rows, -1),
        key_delta.reshape(tok_rows, -1),
        value_delta.reshape(tok_rows, -1),
    )


def rs_kernel(ny, nz, w_ref, out_ref, za, zb, ya, yb, zs, zr, ys, yr):
    me = lax.axis_index("dp")
    my_y, my_z = me // nz, lax.rem(me, nz)
    def at(y, z):
        return lax.rem(y + 2 * ny, ny) * nz + lax.rem(z + 2 * nz, nz)
    sem = pltpu.get_barrier_semaphore()
    for n in (at(my_y, my_z + 1), at(my_y, my_z - 1), at(my_y + 1, my_z), at(my_y - 1, my_z)):
        pl.semaphore_signal(sem, inc=1, device_id={"dp": n}, device_id_type=MESH)
    pl.semaphore_wait(sem, 4)

    cols = w_ref.shape[-1]
    f32 = jnp.float32

    def zid(k):
        return lax.rem(my_z + 2 * nz + k, nz)

    def yid(k):
        return lax.rem(my_y + 2 * ny + k, ny)

    def send(src, dst, ss, rs, dev):
        c = pltpu.make_async_remote_copy(src_ref=src, dst_ref=dst, send_sem=ss, recv_sem=rs,
                                         device_id={"dp": dev}, device_id_type=MESH)
        c.start()
        return c

    zdev = [at(my_y, my_z + 1), at(my_y, my_z - 1)]
    ydev = [at(my_y + 1, my_z), at(my_y - 1, my_z)]
    sign = [1, -1]
    cps = {}
    for i in range(2):
        g = sign[i]
        cps["ya", i, 0] = send(w_ref.at[2 + i, yid(-g)], ya.at[i, 0], ys.at[i, 0], yr.at[i, 0], ydev[i])
    for i in range(2):
        g = sign[i]
        for k in range(ny):
            pass
        cps["za", i, 0] = send(w_ref.at[i, :, zid(-g)], za.at[i, 0], zs.at[i, 0], zr.at[i, 0], zdev[i])
    allc = []

    def z_first(i, s):
        g = sign[i]
        cps["za", i, s].wait_recv()
        c = zid(-g * (2 + s))
        if s < nz - 2:
            za[i, s] = (za[i, s].astype(f32) + w_ref[i, :, c].astype(f32)).astype(jnp.bfloat16)
            cps["za", i, s + 1] = send(za.at[i, s], za.at[i, s + 1], zs.at[i, s + 1], zr.at[i, s + 1], zdev[i])
        else:
            za[i, s] = (za[i, s].astype(f32) + w_ref[i, :, c].astype(f32)).astype(jnp.bfloat16)
            cps["yb", i, 0] = send(za.at[i, s, yid(-g)], yb.at[i, 0], ys.at[i, ny - 1], yr.at[i, ny - 1], ydev[i])

    def y_second(i, s):
        g = sign[i]
        cps["yb", i, s].wait_recv()
        c = yid(-g * (2 + s))
        tot = yb[i, s].astype(f32) + za[i, nz - 2, c].astype(f32)
        if s < ny - 2:
            yb[i, s] = tot.astype(jnp.bfloat16)
            cps["yb", i, s + 1] = send(yb.at[i, s], yb.at[i, s + 1], ys.at[i, ny + s], yr.at[i, ny + s], ydev[i])
        else:
            out_ref[:, i * cols:(i + 1) * cols] = tot

    def y_first(i, s):
        g = sign[i]
        cps["ya", i, s].wait_recv()
        c = yid(-g * (2 + s))
        ya[i, s] = (ya[i, s].astype(f32) + w_ref[2 + i, c].astype(f32)).astype(jnp.bfloat16)
        if s < ny - 2:
            cps["ya", i, s + 1] = send(ya.at[i, s], ya.at[i, s + 1], ys.at[i, s + 1], yr.at[i, s + 1], ydev[i])
        else:
            cps["zb", i, 0] = send(ya.at[i, s, zid(-g)], zb.at[i, 0], zs.at[i, nz - 1], zr.at[i, nz - 1], zdev[i])

    def z_second(i, s):
        g = sign[i]
        cps["zb", i, s].wait_recv()
        c = zid(-g * (2 + s))
        tot = zb[i, s].astype(f32) + ya[i, ny - 2, c].astype(f32)
        if s < nz - 2:
            zb[i, s] = tot.astype(jnp.bfloat16)
            cps["zb", i, s + 1] = send(zb.at[i, s], zb.at[i, s + 1], zs.at[i, nz + s], zr.at[i, nz + s], zdev[i])
        else:
            out_ref[:, (2 + i) * cols:(3 + i) * cols] = tot

    order = []
    za_steps = [(z_first, s) for s in range(nz - 1)] + [(y_second, s) for s in range(ny - 1)]
    ya_steps = [(y_first, s) for s in range(ny - 1)] + [(z_second, s) for s in range(nz - 1)]
    ta = [(s + 1) * 4.0 for s in range(nz - 1)]
    ta += [ta[-1] + (s + 1) * 1.5 for s in range(ny - 1)]
    tb = [(s + 1) * 8.0 for s in range(ny - 1)]
    tb += [tb[-1] + (s + 1) * 1.5 for s in range(nz - 1)]
    plan = [(t, 0, f, s) for t, (f, s) in zip(ta, za_steps)] + [(t, 1, f, s) for t, (f, s) in zip(tb, ya_steps)]
    plan.sort(key=lambda e: (e[0], e[1]))
    for _, _, f, s in plan:
        for i in range(2):
            f(i, s)
    for c in cps.values():
        c.wait_send()

def reduce_scatter(w, ny, nz):
    _, _, _, rows, cols = w.shape
    return pl.pallas_call(
        functools.partial(rs_kernel, ny, nz),
        out_shape=jax.ShapeDtypeStruct((rows, 4 * cols), jnp.float32),
        in_specs=[pl.BlockSpec(memory_space=pltpu.VMEM)],
        out_specs=pl.BlockSpec(memory_space=pltpu.VMEM),
        scratch_shapes=[
            pltpu.VMEM((2, nz - 1, ny, rows, cols), jnp.bfloat16),
            pltpu.VMEM((2, nz - 1, rows, cols), jnp.bfloat16),
            pltpu.VMEM((2, ny - 1, nz, rows, cols), jnp.bfloat16),
            pltpu.VMEM((2, ny - 1, rows, cols), jnp.bfloat16),
            pltpu.SemaphoreType.DMA((2, 2 * (nz - 1))),
            pltpu.SemaphoreType.DMA((2, 2 * (nz - 1))),
            pltpu.SemaphoreType.DMA((2, 2 * (ny - 1))),
            pltpu.SemaphoreType.DMA((2, 2 * (ny - 1))),
        ],
        compiler_params=pltpu.CompilerParams(collective_id=1, has_side_effects=True, vmem_limit_bytes=48 << 20),
        name="weight_grad_rings",
    )(w)


def place_rows(onehot, rows):
    return lax.dot_general(
        onehot, rows, (((1,), (0,)), ((), ())), preferred_element_type=jnp.float32
    ).astype(jnp.bfloat16)


def take_rows(onehot, rows):
    return lax.dot_general(
        onehot, rows, (((0,), (0,)), ((), ())), preferred_element_type=jnp.float32
    ).astype(jnp.bfloat16)


def swap(rows):
    return lax.all_to_all(rows, "dp", split_axis=0, concat_axis=0, tiled=True)


def shards(ny, nz, queries, keys, values, out_grad, out_weight, send_slot, recv_index, packed_doc):
    tok_rows = queries.shape[0]
    peers = ny * nz
    lanes = 2 * tok_rows
    slots = lax.broadcasted_iota(jnp.int32, (lanes, tok_rows), 0)
    send_hot = (slots == send_slot[None, :]).astype(jnp.bfloat16)
    recv_hot = (slots == recv_index[None, :]).astype(jnp.bfloat16)
    grad_moved = swap(place_rows(send_hot, out_grad))
    qkv = place_rows(send_hot, jnp.concatenate([queries, keys, values], axis=1))
    qkv, grad_moved = lax.optimization_barrier((qkv, grad_moved))
    moved = swap(qkv)
    grad_part = take_rows(recv_hot, grad_moved)
    grad_full = lax.all_gather(grad_part, "tensor", axis=1, tiled=True)
    head_grad = lax.dot_general(
        grad_full, out_weight, (((1,), (1,)), ((), ())), preferred_element_type=jnp.float32
    ).astype(jnp.bfloat16)
    pack = take_rows(recv_hot, moved)
    width = queries.shape[1]
    kvw = keys.shape[1]
    attended, query_delta, key_delta, value_delta = attention_backward(
        pack[:, :width], pack[:, width:width + kvw], pack[:, width + kvw:], head_grad, packed_doc
    )
    norm_scale = 1.0 / math.sqrt(tok_rows * peers)
    part = jnp.einsum(
        "tf,tsc->sfc", grad_full, attended.reshape(tok_rows, 4, width // 4),
        preferred_element_type=jnp.float32,
    )
    part = (part * norm_scale).astype(jnp.bfloat16)
    feats = part.shape[1]
    part = part.reshape(4, ny, nz, feats // peers, width // 4)
    back = place_rows(recv_hot, jnp.concatenate([query_delta, key_delta, value_delta], axis=1))
    returned = swap(back)
    weight_grad = reduce_scatter(part, ny, nz)
    home = take_rows(send_hot, returned)
    return home[:, :width], home[:, width:width + kvw], home[:, width + kvw:], weight_grad


def solution(mesh):
    placed = (
        P("dp", "tensor"),
        P("dp", "tensor"),
        P("dp", "tensor"),
        P("dp", "tensor"),
        P("tensor", None),
        P("dp"),
        P("dp"),
        P("dp"),
    )
    nz = 8 if mesh.shape["dp"] % 8 == 0 else 1
    ny = mesh.shape["dp"] // nz
    return jax.shard_map(
        functools.partial(shards, ny, nz),
        mesh=mesh,
        in_specs=placed,
        out_specs=(P("dp", "tensor"), P("dp", "tensor"), P("dp", "tensor"), P("dp", "tensor")),
        check_vma=False,
    )
```

time: 543 us -> 306 us (0.56)
  waiting for transfers between devices: 360 us -> 80 us
  Pallas kernels: 0 us -> 104 us
  local copies, waits for them, and re-layouts: 74.7 us -> 35.7 us
  starting transfers between devices: 50.2 us -> 20.7 us
  matrix products: 27.5 us -> 42.4 us
    all_to_all x7 -> x3, waiting for transfers between devices: 244 us -> 80 us  [swap(): return lax.all_to_all(rows, 'dp', split_axis=0, concat_axis=0, tiled=True)]
    reduce_scatter x1 -> x0, waiting for transfers between devices: 115 us -> none  [shards(): lax.psum_scatter((lax.dot_general(grad_full, attended, (((0,), (0,)), (()...]
    pallas_call x0 -> x1, Pallas kernels: none -> 104 us  [reduce_scatter(): pl.pallas_call(functools.partial(rs_kernel, ny, nz), out_shape=jax.ShapeD...]
    all_to_all x7 -> x3, starting transfers between devices: 50 us -> 20.5 us  [swap(): return lax.all_to_all(rows, 'dp', split_axis=0, concat_axis=0, tiled=True)]
    scatter x7 -> x0, local copies, waits for them, and re-layouts: 29.3 us -> none  [spread(): return holder.at[slots].set(block)]
    gather x7 -> x0, local copies, waits for them, and re-layouts: 22.5 us -> none  [the longest x1 10.6 us: shards(): grad_full = moved[3][recv_index]]
    dot_general x1 -> x7, matrix products: 5.48 us -> 19.8 us  [the longest x3 8.53 us: place_rows(): lax.dot_general(onehot, rows, (((1,), (0,)), ((), ())), preferred_element...]
    convert_element_type x0 -> x1, local copies, waits for them, and re-layouts: none -> 8.61 us  [shards(): part = (part * norm_scale).astype(jnp.bfloat16)]
  transfers between devices with their start and end apart: 9 -> 4, of which waited for: 7 -> 2; matrix products, arithmetic and copies ran while one was open for 13% -> 9% of each run, Pallas kernels for 0% -> 34%
where the time goes in v1:
time: 306 us; the launch traced here: 303 us
  Pallas kernels  104 us (34%)
  waiting for transfers between devices  80 us (26%)
  matrix products  42.4 us (14%)
  local copies, waits for them, and re-layouts  35.7 us (12%)
  starting transfers between devices  20.7 us (7%)
  between operations  14.3 us (5%)
  other arithmetic  6.3 us (2%)
    pallas_call x1, Pallas kernels, reduce_scatter(): pl.pallas_call(functools.partial(rs_kernel, ny, nz), out_shape=jax.ShapeD...  104 us
    all_to_all x3, waiting for transfers between devices, swap(): return lax.all_to_all(rows, 'dp', split_axis=0, concat_axis=0, tiled=True)  80 us
    all_to_all x3, starting transfers between devices, swap(): return lax.all_to_all(rows, 'dp', split_axis=0, concat_axis=0, tiled=True)  20.5 us
    another operation x2, local copies, waits for them, and re-layouts  16.1 us
    unnamed x36, local copies, waits for them, and re-layouts  9.18 us
    convert_element_type x1, local copies, waits for them, and re-layouts, shards(): part = (part * norm_scale).astype(jnp.bfloat16)  8.61 us
    dot_general x3, matrix products, place_rows(): lax.dot_general(onehot, rows, (((1,), (0,)), ((), ())), preferred_element...  8.53 us
    dot_general x1, matrix products, shards(): lax.dot_general(grad_full, out_weight, (((1,), (1,)), ((), ())), preferre...  7.32 us
  transfers between devices with their start and end apart: 4, of which 2 were waited for; matrix products, arithmetic and copies ran while one was open for 9% of the time, Pallas kernels for 34%

profile of v1, /device:TPU:4, one launch (start us, length us, event | category | flops | bytes accessed | tf_op | source)
XLA Modules:
  0.0 303.3 jit_solution(10642174334871658063)
XLA Ops:
  7.2 0.9 copy-done
  8.2 2.3 fusion.11
  10.5 11.5 %all-to-all-start = ((bf16[32,32,384]{2,1,0:T(8,128)(2,1)}), bf16[32,32,384]{2,1,0:T(8,128)(2,1)S(1)}, u32[]{:S(2)}, u32[]{:S(2)}) async-start(bf16[32,32,384]{2,1,0:T(8,128)(2,1)} %bitcast), calls=%async_computation | async-start | bytes 1572864 | tf_op jit(solution)/shard_map/all_to_all | solution.py:197
  22.0 3.1 %convolution_convert_fusion.1 = bf16[1024,1280]{1,0:T(8,128)(2,1)} fusion(bf16[512,128]{1,0:T(8,128)(2,1)S(1)} %copy-done.12, bf16[512,128]{1,0:T(8,128)(2,1)S(1)} %copy-done.13, bf16[512,1024]{1,0:T(8,128)(2,1)S(1)} %copy-done.11, s32[512]{0:T(512)S(1)} %copy-done.15), kind=kOutput, calls=%fused_computation.15 | convolution fusion | flops 1347944448 | bytes 3934208 | tf_op jit(solution)/shard_map/dot_general | solution.py:185
  25.1 20.2 %all-to-all-done = bf16[32,32,384]{2,1,0:T(8,128)(2,1)S(1)} async-done(((bf16[32,32,384]{2,1,0:T(8,128)(2,1)}), bf16[32,32,384]{2,1,0:T(8,128)(2,1)S(1)}, u32[]{:S(2)}, u32[]{:S(2)}) %all-to-all-start) | async-done | bytes 786464 | tf_op jit(solution)/shard_map/all_to_all | solution.py:197
  45.3 0.9 copy-done.8
  46.2 4.7 %all-to-all-start.1 = ((bf16[32,32,1280]{2,1,0:T(8,128)(2,1)}), bf16[32,32,1280]{2,1,0:T(8,128)(2,1)S(1)}, u32[]{:S(2)}, u32[]{:S(2)}) async-start(bf16[32,32,1280]{2,1,0:T(8,128)(2,1)} %bitcast.2), calls=%async_computation.1 | async-start | bytes 5242880 | tf_op jit(solution)/shard_map/all_to_all | solution.py:197
  51.2 2.6 fusion.22
  54.0 59.8 %all-to-all-done.1 = bf16[32,32,1280]{2,1,0:T(8,128)(2,1)S(1)} async-done(((bf16[32,32,1280]{2,1,0:T(8,128)(2,1)}), bf16[32,32,1280]{2,1,0:T(8,128)(2,1)S(1)}, u32[]{:S(2)}, u32[]{:S(2)}) %all-to-all-start.1) | async-done | bytes 2621472 | tf_op jit(solution)/shard_map/all_to_all | solution.py:197
  113.8 1.6 convolution_convert_fusion.3
  116.0 1.6 fusion.5
  117.7 3.2 %copy-done.2 = f32[512,512,8]{1,0,2:T(8,128)} copy-done((f32[512,512,8]{1,0,2:T(8,128)}, f32[512,512,8]{1,0,2:T(8,128)S(1)}, u32[]{:S(2)}) %copy-start.2) | copy-done | bytes 8388632
  120.9 1.8 fusion.4
  122.7 7.3 %convolution_convert_fusion.5 = bf16[512,1024]{1,0:T(8,128)(2,1)S(1)} fusion(bf16[512,3072]{1,0:T(8,128)(2,1)} %all-gather.2.cloned.1.call-done, bf16[1024,3072]{1,0:T(8,128)(2,1)} %param.12), kind=kOutput, calls=%fused_computation.25 | convolution fusion | flops 3221749760 | bytes 10485760 | tf_op jit(solution)/shard_map/dot_general | solution.py:213
  130.0 4.0 %fusion = (f32[8,512]{1,0:T(8,128)S(1)}, f32[512,512,8]{1,0,2:T(8,128)S(1)}) fusion(f32[8,512]{1,0:T(8,128)S(1)} %fusion.4, f32[8,512]{1,0:T(8,128)S(1)} %get-tuple-element.14, f32[512,512,8]{1,0,2:T(8,128)S(1)} %copy-done.3, pred[512,512]{0,1:T(8,128)(4,1)S(1)} %fusion.40, bf16[512,1280]{1,0:T(8,128)(2,1)} %copy-done.6, ...), kind=kOutput, calls=%fused_computation.4 | convolution fusion | flops 549449728 | bytes 18268160 | tf_op jit(solution)/shard_map/tkgd,skd->kgts/dot_general | solution.py:41
  134.1 4.3 %fusion.7 = (bf16[8,512,512]{1,2,0:T(8,128)(2,1)S(1)}, bf16[8,512,512]{1,2,0:T(8,128)(2,1)}) fusion(f32[512,512,8]{1,0,2:T(8,128)S(1)} %get-tuple-element.17, f32[8,512]{1,0:T(8,128)S(1)} %get-tuple-element.16, f32[8,512]{1,0:T(8,128)S(1)} %fusion.4, f32[8,512]{1,0:T(8,128)S(1)} %get-tuple-element.14, f32[512,512,8]{1,0,2:T(8,128)S(1)} %copy-done.3, ...), kind=kLoop, calls=%fused_computation.12 | loop fusion | flops 16777216 | bytes 25477120 | tf_op jit(solution)/shard_map/reshape.18
  138.4 1.9 copy-done.4
  140.3 2.6 multiply_convert_fusion.1
  143.0 8.1 %copy.26 = bf16[8,512,512]{2,0,1:T(8,128)(2,1)} copy(bf16[8,512,512]{1,2,0:T(8,128)(2,1)} %copy-done.4) | data formatting | bytes 8388608 | tf_op jit(solution)/shard_map/reshape.18
  151.3 8.0 %copy.28 = bf16[8,512,512]{2,0,1:T(8,128)(2,1)} copy(bf16[8,512,512]{1,2,0:T(8,128)(2,1)} %get-tuple-element.9) | data formatting | bytes 8388608 | tf_op jit(solution)/shard_map/reshape.28
  159.3 3.1 %fusion.26 = bf16[512,128]{0,1:T(8,128)(2,1)S(1)} fusion(bf16[512,8,128]{2,1,0:T(8,128)(2,1)S(1)} %bitcast.131, bf16[8,512,512]{2,0,1:T(8,128)(2,1)} %copy.28), kind=kOutput, calls=%fused_computation.43 | convolution fusion | flops 536936448 | bytes 5373952 | tf_op jit(solution)/shard_map/kgts,tkgd->skd/dot_general | solution.py:54
  162.8 0.8 fusion.27
  163.8 3.1 %convolution_convert_fusion = bf16[1024,1280]{1,0:T(8,128)(2,1)} fusion(bf16[512,128]{0,1:T(8,128)(2,1)S(1)} %fusion.26, bf16[512,128]{0,1:T(8,128)(2,1)S(1)} %fusion.27, bf16[512,1024]{0,1:T(8,128)(2,1)S(1)} %bitcast.136, s32[512]{0:T(512)S(1)} %copy-done.14), kind=kOutput, calls=%fused_computation.14 | convolution fusion | flops 1347944448 | bytes 3934208 | tf_op jit(solution)/shard_map/dot_general | solution.py:185
  166.9 4.3 %all-to-all-start.2 = ((bf16[32,32,1280]{2,1,0:T(8,128)(2,1)}), bf16[32,32,1280]{2,1,0:T(8,128)(2,1)S(1)}, u32[]{:S(2)}, u32[]{:S(2)}) async-start(bf16[32,32,1280]{2,1,0:T(8,128)(2,1)} %bitcast.134), calls=%async_computation.2 | async-start | bytes 5242880 | tf_op jit(solution)/shard_map/all_to_all | solution.py:197
  171.2 3.1 %convolution_convert_fusion.4 = bf16[128,8,512]{2,0,1:T(8,128)(2,1)S(1)} fusion(bf16[8,512,512]{1,2,0:T(8,128)(2,1)} %get-tuple-element.9, bf16[512,1280]{1,0:T(8,128)(2,1)} %copy-done.6), kind=kOutput, calls=%fused_computation.24 | convolution fusion | flops 537395200 | bytes 5373952 | tf_op jit(solution)/shard_map/kgts,skd->tkgd/dot_general | solution.py:37
  174.5 5.4 %fusion.6 = bf16[4,3072,256]{1,2,0:T(8,128)(2,1)} fusion(bf16[512,4,256]{0,2,1:T(8,128)(2,1)S(1)} %bitcast.137, bf16[512,3072]{1,0:T(8,128)(2,1)S(1)} %copy-done.10), kind=kOutput, calls=%fused_computation.11 | convolution fusion | flops 3227516928 | bytes 10485760 | tf_op jit(solution)/shard_map/tf,tsc->sfc/dot_general | solution.py:223
  179.9 8.6 %copy.22 = bf16[4,3072,256]{2,1,0:T(8,128)(2,1)} copy(bf16[4,3072,256]{1,2,0:T(8,128)(2,1)} %fusion.6) | data formatting | bytes 12582912 | tf_op jit(solution)/shard_map/convert_element_type | solution.py:227
  188.5 103.8 %weight_grad_rings.1 = f32[96,1024]{1,0:T(8,128)S(1)} custom-call(bf16[4,4,8,96,256]{4,3,2,1,0:T(8,128)(2,1)} %bitcast.129), custom_call_target="tpu_custom_call" | custom-call | tf_op jit(solution)/shard_map/weight_grad_rings/pallas_call | solution.py:164
  292.3 1.6 convolution_convert_fusion.2
  293.9 0.7 fusion.43
  294.6 1.1 slice.27
  295.7 0.7 copy.52
  (36 shorter events, 1.9 us)
Async XLA Ops:
  7.2 1.0 copy-start
  7.2 14.8 %copy-start.15 = (s32[512]{0:T(512)S(1)}, s32[512]{0:T(512)}, u32[]{:S(2)}) copy-start(s32[512]{0:T(512)} %param.13) | copy-start | bytes 6148
  7.2 14.8 %copy-start.12 = (bf16[512,128]{1,0:T(8,128)(2,1)S(1)}, bf16[512,128]{1,0:T(8,128)(2,1)}, u32[]{:S(2)}) copy-start(bf16[512,128]{1,0:T(8,128)(2,1)} %param.10) | copy-start | bytes 393220
  7.2 14.8 %copy-start.13 = (bf16[512,128]{1,0:T(8,128)(2,1)S(1)}, bf16[512,128]{1,0:T(8,128)(2,1)}, u32[]{:S(2)}) copy-start(bf16[512,128]{1,0:T(8,128)(2,1)} %param.9) | copy-start | bytes 393220
  7.2 14.8 %copy-start.11 = (bf16[512,1024]{1,0:T(8,128)(2,1)S(1)}, bf16[512,1024]{1,0:T(8,128)(2,1)}, u32[]{:S(2)}) copy-start(bf16[512,1024]{1,0:T(8,128)(2,1)} %param.8) | copy-start | bytes 3145732
  10.5 34.9 %all-to-all-start = ((bf16[32,32,384]{2,1,0:T(8,128)(2,1)}), bf16[32,32,384]{2,1,0:T(8,128)(2,1)S(1)}, u32[]{:S(2)}, u32[]{:S(2)}) async-start(bf16[32,32,384]{2,1,0:T(8,128)(2,1)} %bitcast), calls=%async_computation | async-start | bytes 1572864 | tf_op jit(solution)/shard_map/all_to_all | solution.py:197
  25.1 26.1 %copy-start.14 = (s32[512]{0:T(512)S(1)}, s32[512]{0:T(512)}, u32[]{:S(2)}) copy-start(s32[512]{0:T(512)} %param.14) | copy-start | bytes 6148
  45.3 0.9 copy-start.8
  45.3 8.5 %copy-start.9 = (s32[512]{0:T(512)S(1)}, s32[512]{0:T(512)}, u32[]{:S(2)}) copy-start(s32[512]{0:T(512)} %param.15) | copy-start | bytes 6148
  46.2 67.6 %all-to-all-start.1 = ((bf16[32,32,1280]{2,1,0:T(8,128)(2,1)}), bf16[32,32,1280]{2,1,0:T(8,128)(2,1)S(1)}, u32[]{:S(2)}, u32[]{:S(2)}) async-start(bf16[32,32,1280]{2,1,0:T(8,128)(2,1)} %bitcast.2), calls=%async_computation.1 | async-start | bytes 5242880 | tf_op jit(solution)/shard_map/all_to_all | solution.py:197
  50.9 71.8 %all-gather.2.cloned.1.call-start = ((), (), s32[]{:S(2)}) async-start(), calls=%async_computation.3 | async-start | bytes 3538944 | tf_op jit(solution)/shard_map/all_gather | solution.py:212
  115.4 2.2 copy-start.6
  117.6 3.3 %copy-start.2 = (f32[512,512,8]{1,0,2:T(8,128)}, f32[512,512,8]{1,0,2:T(8,128)S(1)}, u32[]{:S(2)}) copy-start(f32[512,512,8]{1,0,2:T(8,128)S(1)} %get-tuple-element.15) | copy-start | bytes 25165828
  122.7 7.3 %copy-start.3 = (f32[512,512,8]{1,0,2:T(8,128)S(1)}, f32[512,512,8]{1,0,2:T(8,128)}, u32[]{:S(2)}) copy-start(f32[512,512,8]{1,0,2:T(8,128)} %copy-done.2) | copy-start | bytes 25165828
  138.4 1.9 copy-start.4
  159.3 3.4 %copy-start.5 = (bf16[8,512,512]{2,0,1:T(8,128)(2,1)S(1)}, bf16[8,512,512]{2,0,1:T(8,128)(2,1)}, u32[]{:S(2)}) copy-start(bf16[8,512,512]{2,0,1:T(8,128)(2,1)} %copy.26) | copy-start | bytes 12582916
  162.5 1.3 copy-start.7
  166.9 125.4 %all-to-all-start.2 = ((bf16[32,32,1280]{2,1,0:T(8,128)(2,1)}), bf16[32,32,1280]{2,1,0:T(8,128)(2,1)S(1)}, u32[]{:S(2)}, u32[]{:S(2)}) async-start(bf16[32,32,1280]{2,1,0:T(8,128)(2,1)} %bitcast.134), calls=%async_computation.2 | async-start | bytes 5242880 | tf_op jit(solution)/shard_map/all_to_all | solution.py:197
  171.2 3.2 %copy-start.10 = (bf16[512,3072]{1,0:T(8,128)(2,1)S(1)}, bf16[512,3072]{1,0:T(8,128)(2,1)}, u32[]{:S(2)}) copy-start(bf16[512,3072]{1,0:T(8,128)(2,1)} %all-gather.2.cloned.1.call-done) | copy-start | bytes 9437188
  292.3 4.2 %copy-start.1 = (bf16[512,384]{1,0:T(8,128)(2,1)S(1)}, bf16[512,384]{1,0:T(8,128)(2,1)}, u32[]{:S(2)}) copy-start(bf16[512,384]{1,0:T(8,128)(2,1)} %param.11) | copy-start | bytes 1179652
Sparse Core Ops, SparseCore 0:
  54.2 30.1 all-gather.1

commit v2 on v0

v2 whole, which is shorter than its diff:
```python
import functools
import math

import jax
import jax.numpy as jnp
from jax import lax
from jax.experimental import pallas as pl
from jax.experimental.pallas import tpu as pltpu
from jax.sharding import PartitionSpec as P

MESH = pl.DeviceIdType.MESH
BF = jnp.bfloat16
F32 = jnp.float32
CAP = 32
HEAD_DIM = 128
NY = 4
NZ = 8
NX = 4
NDP = NY * NZ
TOK = 512
LANES = NDP * CAP
BLK = 256
NB = 4
PART = 384
FEAT = 3072
ROWS = FEAT // NDP
SLAB = NZ * ROWS


def nn(a, b):
    return lax.dot_general(a, b, (((1,), (0,)), ((), ())), preferred_element_type=F32)


def nt(a, b):
    return lax.dot_general(a, b, (((1,), (1,)), ((), ())), preferred_element_type=F32)


def kernel(
    q_ref, k_ref, v_ref, g_ref, w_ref, ss_row, ss_col, ri_row, ri_col, doc_row, doc_col,
    qg_ref, kg_ref, vg_ref, wg_ref,
    send_g, recv_g, send_x, recv_x, back, home,
    sel_r, sel_rt, gt, bias, kv, kvt, dkv, hgt, att, dqt,
    part, ya, yb, yc, yt, za, zb,
    sem_gs, sem_gr, sem_xs, sem_xr, sem_bs, sem_br, sem_as, sem_ar, sem_ys, sem_yr, sem_zs, sem_zr,
):
    me = lax.axis_index("dp")
    tp = lax.axis_index("tensor")
    my_y, my_z = me // NZ, lax.rem(me, NZ)
    my_x, core = tp // 2, lax.rem(tp, 2)

    def peer(k):
        return lax.rem(my_y + k // NZ, NY) * NZ + lax.rem(my_z + 3 * k, NZ)

    def x_dev(dx, c):
        return lax.rem(my_x + dx + NX, NX) * 2 + c

    def dp_dev(dy, dz):
        return lax.rem(my_y + dy + NY, NY) * NZ + lax.rem(my_z + dz + NZ, NZ)

    barrier = pltpu.get_barrier_semaphore()

    def greet(k, _):
        pl.semaphore_signal(barrier, inc=1, device_id={"dp": peer(k)}, device_id_type=MESH)
        return 0

    lax.fori_loop(1, NDP, greet, 0)
    for t in (x_dev(1, core), x_dev(-1, core), x_dev(0, 1 - core)):
        pl.semaphore_signal(barrier, inc=1, device_id={"tensor": t}, device_id_type=MESH)

    slot_rows = lax.broadcasted_iota(jnp.int32, (LANES, TOK), 0)
    sel_rt[...] = (slot_rows == ss_row[...]).astype(BF)
    send_g[...] = nn(sel_rt[...], g_ref[...]).astype(BF)
    pl.semaphore_wait(barrier, NDP - 1 + 3)

    def rows_of(d):
        return pl.ds(pl.multiple_of(d * CAP, CAP), CAP)

    def exchange(src, dst, s_sem, r_sem):
        def one(k, _):
            d = peer(k)
            pltpu.make_async_remote_copy(
                src_ref=src.at[rows_of(d)], dst_ref=dst.at[rows_of(me)],
                send_sem=s_sem, recv_sem=r_sem, device_id={"dp": d}, device_id_type=MESH,
            ).start()
            return 0

        lax.fori_loop(1, NDP, one, 0)
        dst[rows_of(me)] = src[rows_of(me)]

    def drain(ref, sem):
        whole = ref.at[pl.ds(0, LANES - CAP)]
        pltpu.make_async_copy(whole, whole, sem).wait()

    exchange(send_g, recv_g, sem_gs, sem_gr)
    kv_in = jnp.concatenate([k_ref[...], v_ref[...]], axis=1)
    send_x[NB] = nn(sel_rt[...], kv_in).astype(BF)
    exchange(send_x.at[NB], recv_x.at[NB], sem_xs.at[NB], sem_xr.at[NB])

    def push_q(j, _):
        cols = pl.ds(pl.multiple_of(j * BLK, BLK), BLK)
        send_x[j] = nn(sel_rt[...], q_ref[:, cols]).astype(BF)
        exchange(send_x.at[j], recv_x.at[j], sem_xs.at[j], sem_xr.at[j])
        return 0

    lax.fori_loop(0, NB, push_q, 0)

    slot_cols = lax.broadcasted_iota(jnp.int32, (TOK, LANES), 1)
    sel_r[...] = (slot_cols == ri_col[...]).astype(BF)
    sel_rt[...] = (slot_rows == ri_row[...]).astype(BF)
    key_at = lax.broadcasted_iota(jnp.int32, (TOK, TOK), 0)
    query_at = lax.broadcasted_iota(jnp.int32, (TOK, TOK), 1)
    seen = (doc_col[...] == doc_row[...]) & (key_at <= query_at)
    bias[...] = jnp.where(seen, 0.0, -1e30).astype(F32)
    dkv[...] = jnp.zeros_like(dkv)

    drain(recv_g, sem_gr)

    def feats(t, lo=0, n=PART):
        return pl.ds(pl.multiple_of(t * PART + lo, 16), n)

    mine = nn(sel_r[...], recv_g[...]).T.astype(BF)
    gt[feats(tp)] = mine

    def ring(idx, t, lo, n, dev):
        c = pltpu.make_async_remote_copy(
            src_ref=gt.at[feats(t, lo, n)], dst_ref=gt.at[feats(t, lo, n)],
            send_sem=sem_as.at[idx], recv_sem=sem_ar.at[idx],
            device_id={"tensor": dev}, device_id_type=MESH,
        )
        c.start()
        return c

    right, left, twin = x_dev(1, core), x_dev(-1, core), x_dev(0, 1 - core)
    far = x_dev(2, core)
    half = PART // 2
    cps = [
        ring(0, tp, 0, PART, right),
        ring(1, tp, 0, PART, left),
        ring(2, tp, 0, PART, twin),
    ]

    def arrived(idx, t, lo, n):
        ref = gt.at[feats(t, lo, n)]
        pltpu.make_async_copy(ref, ref, sem_ar.at[idx]).wait()

    arrived(0, left, 0, PART)
    cps.append(ring(3, left, 0, half, right))
    cps.append(ring(4, left, 0, PART, twin))
    arrived(1, right, 0, PART)
    cps.append(ring(5, right, half, half, left))
    cps.append(ring(6, right, 0, PART, twin))
    arrived(3, far, 0, half)
    arrived(5, far, half, half)
    cps.append(ring(7, far, 0, PART, twin))

    drain(recv_x.at[NB], sem_xr.at[NB])
    kv_f = nn(sel_r[...], recv_x[NB])
    kv[...] = kv_f.astype(BF)
    kvt[...] = kv_f.T.astype(BF)

    arrived(2, x_dev(0, 1 - core), 0, PART)
    arrived(4, x_dev(-1, 1 - core), 0, PART)
    arrived(6, x_dev(1, 1 - core), 0, PART)
    arrived(7, x_dev(2, 1 - core), 0, PART)

    inv = 1.0 / math.sqrt(HEAD_DIM)
    norm = 1.0 / math.sqrt(TOK * NDP)
    HALF = TOK // 2

    def head_block(j):
        rows = pl.ds(pl.multiple_of(j * BLK, BLK), BLK)
        hgt[...] = nn(w_ref[rows, :], gt[...]).astype(BF)
        qp = nn(sel_r[...], recv_x[j]).astype(BF)
        for h in range(2):
            hs = slice(h * HEAD_DIM, (h + 1) * HEAD_DIM)
            for b in range(2):
                kn = HALF * (b + 1)
                ps = slice(b * HALF, (b + 1) * HALF)
                qh = qp[ps, hs]
                keys, vals = kv[:kn, :HEAD_DIM], kv[:kn, HEAD_DIM:]
                s = nt(keys, qh) + bias[:kn, ps]
                top = jnp.max(s, axis=0, keepdims=True)
                e = jnp.exp((s - top) * inv)
                soft = e * (1.0 / jnp.sum(e, axis=0, keepdims=True))
                soft_half = soft.astype(BF)
                att[hs, ps] = nn(kvt[HEAD_DIM:, :kn], soft_half).astype(BF)
                hg = hgt[hs, ps]
                dp_ = nn(vals, hg)
                inner = jnp.sum(soft * dp_, axis=0, keepdims=True)
                ds = (soft * (dp_ - inner)).astype(BF)
                dqt[hs, ps] = (nn(kvt[:HEAD_DIM, :kn], ds) * inv).astype(BF)
                dkv[:kn, :HEAD_DIM] += nn(ds, qh)
                dkv[:kn, HEAD_DIM:] += nt(soft_half, hg)

        def weight_slab(y, _):
            rows = pl.ds(pl.multiple_of(y * SLAB, SLAB), SLAB)
            part[j, y] = (nt(gt[rows, :], att[...]) * norm).astype(BF).reshape(NZ, ROWS, BLK)
            return 0

        lax.fori_loop(0, NY, weight_slab, 0)

    def yid(k):
        return lax.rem(my_y + k + 2 * NY, NY)

    def zid(k):
        return lax.rem(my_z + k + 2 * NZ, NZ)

    def send(src, dst, ss, rs, dev):
        pltpu.make_async_remote_copy(
            src_ref=src, dst_ref=dst, send_sem=ss, recv_sem=rs,
            device_id={"dp": dev}, device_id_type=MESH,
        ).start()

    def landed(ref, sem):
        pltpu.make_async_copy(ref, ref, sem).wait()

    def sgn(j):
        return 1 - 2 * lax.rem(j, 2)

    def y_start(j):
        g = sgn(j)
        send(part.at[j, yid(2 * g)], ya.at[j], sem_ys.at[j, 0], sem_yr.at[j, 0], dp_dev(g, 0))
        send(part.at[j, yid(-g)], yb.at[j], sem_ys.at[j, 1], sem_yr.at[j, 1], dp_dev(-g, 0))

    def y_next(j):
        g = sgn(j)
        landed(ya.at[j], sem_yr.at[j, 0])
        ya[j] = (ya[j].astype(F32) + part[j, yid(g)].astype(F32)).astype(BF)
        send(ya.at[j], yc.at[j], sem_ys.at[j, 2], sem_yr.at[j, 2], dp_dev(g, 0))

    def y_end(j):
        g = sgn(j)
        landed(yb.at[j], sem_yr.at[j, 1])
        landed(yc.at[j], sem_yr.at[j, 2])
        yt[j] = (yb[j].astype(F32) + yc[j].astype(F32) + part[j, my_y].astype(F32)).astype(BF)
        send(yt.at[j, zid(4 * g)], za.at[j, 0], sem_zs.at[j, 0], sem_zr.at[j, 0], dp_dev(0, g))
        send(yt.at[j, zid(-3 * g)], zb.at[j, 0], sem_zs.at[j, 4], sem_zr.at[j, 4], dp_dev(0, -g))

    def z_next(j, s):
        g = sgn(j)
        landed(za.at[j, s], sem_zr.at[j, s])
        if s < 3:
            za[j, s] = (za[j, s].astype(F32) + yt[j, zid((3 - s) * g)].astype(F32)).astype(BF)
            send(za.at[j, s], za.at[j, s + 1], sem_zs.at[j, s + 1], sem_zr.at[j, s + 1], dp_dev(0, g))
        if s < 3:
            landed(zb.at[j, s], sem_zr.at[j, 4 + s])
        if s < 2:
            zb[j, s] = (zb[j, s].astype(F32) + yt[j, zid((s - 2) * g)].astype(F32)).astype(BF)
            send(zb.at[j, s], zb.at[j, s + 1], sem_zs.at[j, 5 + s], sem_zr.at[j, 5 + s], dp_dev(0, -g))
        if s == 3:
            cols = pl.ds(pl.multiple_of(j * BLK, BLK), BLK)
            wg_ref[:, cols] = za[j, 3].astype(F32) + zb[j, 2].astype(F32) + yt[j, my_z].astype(F32)

    def step(j, _):
        drain(recv_x.at[j], sem_xr.at[j])
        head_block(j)
        y_start(j)
        back[j] = nt(sel_rt[...], dqt[...]).astype(BF)
        exchange(back.at[j], home.at[j], sem_bs.at[j], sem_br.at[j])

        @pl.when(j >= 1)
        def _():
            y_next(j - 1)

        @pl.when(j >= 2)
        def _():
            y_end(j - 2)

        return 0

    lax.fori_loop(0, NB, step, 0)

    lane = lax.broadcasted_iota(jnp.int32, (TOK, 2 * HEAD_DIM), 1)
    dkv_h = (dkv[...] * jnp.where(lane < HEAD_DIM, inv, 1.0)).astype(BF)
    back[NB] = nn(sel_rt[...], dkv_h).astype(BF)
    exchange(back.at[NB], home.at[NB], sem_bs.at[NB], sem_br.at[NB])

    sel_r[...] = (slot_cols == ss_col[...]).astype(BF)
    y_next(NB - 1)
    for s in range(3):
        z_next(0, s)
    y_end(NB - 2)
    z_next(0, 3)
    for s in range(4):
        z_next(1, s)

    def settle(j):
        drain(home.at[j], sem_br.at[j])
        return nn(sel_r[...], home[j]).astype(BF)

    qg_ref[:, 0:BLK] = settle(0)
    y_end(NB - 1)
    z_next(2, 0)
    qg_ref[:, BLK:2 * BLK] = settle(1)
    z_next(2, 1)
    z_next(3, 0)
    z_next(2, 2)
    z_next(3, 1)
    z_next(2, 3)
    z_next(3, 2)
    z_next(3, 3)
    qg_ref[:, 2 * BLK:3 * BLK] = settle(2)
    qg_ref[:, 3 * BLK:] = settle(3)
    got = settle(NB)
    kg_ref[...] = got[:, :HEAD_DIM]
    vg_ref[...] = got[:, HEAD_DIM:]

    drain(send_g, sem_gs)

    def sent(j, _):
        drain(send_x.at[j], sem_xs.at[j])
        drain(back.at[j], sem_bs.at[j])
        return 0

    lax.fori_loop(0, NB + 1, sent, 0)
    for c in cps:
        c.wait_send()

    def ring_sent(j, _):
        landed(ya.at[j], sem_ys.at[j, 0])
        landed(ya.at[j], sem_ys.at[j, 1])
        landed(ya.at[j], sem_ys.at[j, 2])
        for s in range(7):
            landed(za.at[j, 0], sem_zs.at[j, s])
        return 0

    lax.fori_loop(0, NB, ring_sent, 0)


def shards(queries, keys, values, out_grad, out_weight, send_slot, recv_index, packed_doc):
    row = lambda a: a.reshape(1, TOK)
    col = lambda a: a.reshape(TOK, 1)
    vmem = pl.BlockSpec(memory_space=pltpu.VMEM)
    dma = pltpu.SemaphoreType.DMA
    return pl.pallas_call(
        kernel,
        out_shape=(
            jax.ShapeDtypeStruct((TOK, NB * BLK), BF),
            jax.ShapeDtypeStruct((TOK, HEAD_DIM), BF),
            jax.ShapeDtypeStruct((TOK, HEAD_DIM), BF),
            jax.ShapeDtypeStruct((ROWS, NB * BLK), F32),
        ),
        in_specs=[vmem] * 11,
        out_specs=(vmem,) * 4,
        scratch_shapes=[
            pltpu.VMEM((LANES, PART), BF),
            pltpu.VMEM((LANES, PART), BF),
            pltpu.VMEM((NB + 1, LANES, BLK), BF),
            pltpu.VMEM((NB + 1, LANES, BLK), BF),
            pltpu.VMEM((NB + 1, LANES, BLK), BF),
            pltpu.VMEM((NB + 1, LANES, BLK), BF),
            pltpu.VMEM((TOK, LANES), BF),
            pltpu.VMEM((LANES, TOK), BF),
            pltpu.VMEM((FEAT, TOK), BF),
            pltpu.VMEM((TOK, TOK), F32),
            pltpu.VMEM((TOK, BLK), BF),
            pltpu.VMEM((BLK, TOK), BF),
            pltpu.VMEM((TOK, BLK), F32),
            pltpu.VMEM((BLK, TOK), BF),
            pltpu.VMEM((BLK, TOK), BF),
            pltpu.VMEM((BLK, TOK), BF),
            pltpu.VMEM((NB, NY, NZ, ROWS, BLK), BF),
            pltpu.VMEM((NB, NZ, ROWS, BLK), BF),
            pltpu.VMEM((NB, NZ, ROWS, BLK), BF),
            pltpu.VMEM((NB, NZ, ROWS, BLK), BF),
            pltpu.VMEM((NB, NZ, ROWS, BLK), BF),
            pltpu.VMEM((NB, 4, ROWS, BLK), BF),
            pltpu.VMEM((NB, 3, ROWS, BLK), BF),
            dma, dma,
            dma((NB + 1,)), dma((NB + 1,)),
            dma((NB + 1,)), dma((NB + 1,)),
            dma((8,)), dma((8,)),
            dma((NB, 3)), dma((NB, 3)),
            dma((NB, 7)), dma((NB, 7)),
        ],
        compiler_params=pltpu.CompilerParams(
            collective_id=1, has_side_effects=True, vmem_limit_bytes=60 << 20
        ),
        name="packed_attention_backward",
    )(
        queries, keys, values, out_grad, out_weight,
        row(send_slot), col(send_slot), row(recv_index), col(recv_index),
        row(packed_doc), col(packed_doc),
    )


def solution(mesh):
    both = P("dp", "tensor")
    return jax.shard_map(
        shards,
        mesh=mesh,
        in_specs=(both, both, both, both, P("tensor", None), P("dp"), P("dp"), P("dp")),
        out_specs=(both, both, both, both),
        check_vma=False,
    )
```

time: 543 us -> 196 us (0.36); the launches traced: 536 us -> 196 us
  waiting for transfers between devices: 360 us -> 0 us
  Pallas kernels: 0 us -> 184 us
  local copies, waits for them, and re-layouts: 74.7 us -> 11.8 us
  starting transfers between devices: 50.2 us -> 0 us
  matrix products: 27.5 us -> 0 us
  between operations: 14.8 us -> 0.64 us
  other arithmetic: 8.74 us -> 0 us
    all_to_all x7 -> x0, waiting for transfers between devices: 244 us -> none  [the longest x1 125 us: shards(): lax.all_to_all(spread(grad_slab, send_slot, lanes), 'dp', split_axis=0, c...]
    pallas_call x0 -> x1, Pallas kernels: none -> 184 us  [shards(): pl.pallas_call(kernel, out_shape=(jax.ShapeDtypeStruct((TOK, NB * BLK), B...]
    reduce_scatter x1 -> x0, waiting for transfers between devices: 115 us -> none  [shards(): lax.psum_scatter((lax.dot_general(grad_full, attended, (((0,), (0,)), (()...]
    all_to_all x7 -> x0, starting transfers between devices: 50 us -> none  [the longest x1 11.5 us: shards(): lax.all_to_all(spread(keys, send_slot, lanes), 'dp', split_axis=0, concat...]
    scatter x7 -> x0, local copies, waits for them, and re-layouts: 29.3 us -> none  [spread(): return holder.at[slots].set(block)]
    dot_general x8 -> x0, matrix products: 27.5 us -> none  [the longest x1 7.32 us: shards(): lax.dot_general(grad_full, out_weight, (((1,), (1,)), ((), ())), preferre...]
    gather x7 -> x0, local copies, waits for them, and re-layouts: 22.5 us -> none  [the longest x1 10.6 us: shards(): grad_full = moved[3][recv_index]]
    another operation x2 -> x0, local copies, waits for them, and re-layouts: 16.2 us -> none
  transfers between devices with their start and end apart: 9 -> 0, of which waited for: 7 -> 0; matrix products, arithmetic and copies ran while one was open for 13% -> 0% of each run, Pallas kernels for 0% -> 0%
where the time goes in v2:
time: 196 us
  Pallas kernels  184 us (94%)
  local copies, waits for them, and re-layouts  11.8 us (6%)
    pallas_call x1, Pallas kernels, shards(): pl.pallas_call(kernel, out_shape=(jax.ShapeDtypeStruct((TOK, NB * BLK), B...  184 us
    unnamed x4, local copies, waits for them, and re-layouts  7.16 us
    reshape x3, local copies, waits for them, and re-layouts, shards(): col = lambda a: a.reshape(TOK, 1)  4.6 us

profile of v2, /device:TPU:4, one launch (start us, length us, event | category | flops | bytes accessed | tf_op | source)
XLA Modules:
  0.0 196.0 jit_solution(6762893446796438165)
XLA Ops:
  0.6 1.5 copy.14.doc_col
  2.2 1.5 copy.13.ri_col
  3.7 1.5 copy.12.ss_col
  5.2 183.6 %packed_attention_backward.1 = (bf16[512,1024]{1,0:T(8,128)(2,1)}, bf16[512,128]{1,0:T(8,128)(2,1)}, bf16[512,128]{1,0:T(8,128)(2,1)}, f32[96,1024]{1,0:T(8,128)}) custom-call(bf16[512,1024]{1,0:T(8,128)(2,1)} %q_ref.1, bf16[512,128]{1,0:T(8,128)(2,1)} %k_ref.1, bf16[512,128]{1,0:T(8,128)(2,1)} %v_ref.1, bf16[512,384]{1,0:T(8,128)(2,1)} %g_ref.1, ...), custom_call_target="tpu_custom_call" | custom-call | tf_op jit(solution)/shard_map/packed_attention_backward/pallas_call | solution.py:335
  188.8 2.3 %copy.19 = bf16[512,1024]{1,0:T(8,128)(2,1)} copy(bf16[512,1024]{1,0:T(8,128)(2,1)} %get-tuple-element.8) | data formatting | bytes 2097152
  191.1 1.6 copy.20
  192.6 1.6 copy.21
  194.2 1.8 copy.22

commit v3 on v2

--- a/solution.py
+++ b/solution.py
@@ -35,9 +35,14 @@
     return lax.dot_general(a, b, (((1,), (1,)), ((), ())), preferred_element_type=F32)
 
 
+def column(row_ref):
+    return jnp.broadcast_to(row_ref[...], (HEAD_DIM, TOK)).T[:, :1]
+
+
 def kernel(
-    q_ref, k_ref, v_ref, g_ref, w_ref, ss_row, ss_col, ri_row, ri_col, doc_row, doc_col,
+    q_hbm, k_hbm, v_hbm, g_ref, w_hbm, ss_row, ri_row, doc_row,
     qg_ref, kg_ref, vg_ref, wg_ref,
+    q_ref, k_ref, v_ref, w_ref, sem_in,
     send_g, recv_g, send_x, recv_x, back, home,
     sel_r, sel_rt, gt, bias, kv, kvt, dkv, hgt, att, dqt,
     part, ya, yb, yc, yt, za, zb,
@@ -57,6 +62,15 @@
     def dp_dev(dy, dz):
         return lax.rem(my_y + dy + NY, NY) * NZ + lax.rem(my_z + dz + NZ, NZ)
 
+    loads = [
+        pltpu.make_async_copy(src, dst, sem_in.at[i])
+        for i, (src, dst) in enumerate(
+            ((k_hbm, k_ref), (v_hbm, v_ref), (q_hbm, q_ref), (w_hbm, w_ref))
+        )
+    ]
+    for c in loads:
+        c.start()
+
     barrier = pltpu.get_barrier_semaphore()
 
     def greet(k, _):
@@ -92,6 +106,8 @@
         pltpu.make_async_copy(whole, whole, sem).wait()
 
     exchange(send_g, recv_g, sem_gs, sem_gr)
+    loads[0].wait()
+    loads[1].wait()
     kv_in = jnp.concatenate([k_ref[...], v_ref[...]], axis=1)
     send_x[NB] = nn(sel_rt[...], kv_in).astype(BF)
     exchange(send_x.at[NB], recv_x.at[NB], sem_xs.at[NB], sem_xr.at[NB])
@@ -102,14 +118,15 @@
         exchange(send_x.at[j], recv_x.at[j], sem_xs.at[j], sem_xr.at[j])
         return 0
 
+    loads[2].wait()
     lax.fori_loop(0, NB, push_q, 0)
 
     slot_cols = lax.broadcasted_iota(jnp.int32, (TOK, LANES), 1)
-    sel_r[...] = (slot_cols == ri_col[...]).astype(BF)
+    sel_r[...] = (slot_cols == column(ri_row)).astype(BF)
     sel_rt[...] = (slot_rows == ri_row[...]).astype(BF)
     key_at = lax.broadcasted_iota(jnp.int32, (TOK, TOK), 0)
     query_at = lax.broadcasted_iota(jnp.int32, (TOK, TOK), 1)
-    seen = (doc_col[...] == doc_row[...]) & (key_at <= query_at)
+    seen = (column(doc_row) == doc_row[...]) & (key_at <= query_at)
     bias[...] = jnp.where(seen, 0.0, -1e30).astype(F32)
     dkv[...] = jnp.zeros_like(dkv)
 
@@ -163,6 +180,7 @@
     arrived(6, x_dev(1, 1 - core), 0, PART)
     arrived(7, x_dev(2, 1 - core), 0, PART)
 
+    loads[3].wait()
     inv = 1.0 / math.sqrt(HEAD_DIM)
     norm = 1.0 / math.sqrt(TOK * NDP)
     HALF = TOK // 2
@@ -262,10 +280,6 @@
         def _():
             y_next(j - 1)
 
-        @pl.when(j >= 2)
-        def _():
-            y_end(j - 2)
-
         return 0
 
     lax.fori_loop(0, NB, step, 0)
@@ -275,32 +289,34 @@
     back[NB] = nn(sel_rt[...], dkv_h).astype(BF)
     exchange(back.at[NB], home.at[NB], sem_bs.at[NB], sem_br.at[NB])
 
-    sel_r[...] = (slot_cols == ss_col[...]).astype(BF)
-    y_next(NB - 1)
-    for s in range(3):
-        z_next(0, s)
-    y_end(NB - 2)
-    z_next(0, 3)
-    for s in range(4):
-        z_next(1, s)
-
+    sel_r[...] = (slot_cols == column(ss_row)).astype(BF)
     def settle(j):
         drain(home.at[j], sem_br.at[j])
         return nn(sel_r[...], home[j]).astype(BF)
 
-    qg_ref[:, 0:BLK] = settle(0)
-    y_end(NB - 1)
+    y_end(0)
+    y_end(1)
+    z_next(0, 0)
+    y_next(3)
+    y_end(2)
+    z_next(1, 0)
+    z_next(0, 1)
+    z_next(1, 1)
     z_next(2, 0)
-    qg_ref[:, BLK:2 * BLK] = settle(1)
+    z_next(0, 2)
+    y_end(3)
+    z_next(1, 2)
     z_next(2, 1)
+    z_next(0, 3)
     z_next(3, 0)
+    z_next(1, 3)
     z_next(2, 2)
     z_next(3, 1)
     z_next(2, 3)
     z_next(3, 2)
     z_next(3, 3)
-    qg_ref[:, 2 * BLK:3 * BLK] = settle(2)
-    qg_ref[:, 3 * BLK:] = settle(3)
+    for j in range(NB):
+        qg_ref[:, j * BLK:(j + 1) * BLK] = settle(j)
     got = settle(NB)
     kg_ref[...] = got[:, :HEAD_DIM]
     vg_ref[...] = got[:, HEAD_DIM:]
@@ -327,12 +343,17 @@
     lax.fori_loop(0, NB, ring_sent, 0)
 
 
+def hand_on(*refs):
+    for src, dst in zip(refs[:4], refs[4:]):
+        dst[...] = src[...]
+
+
 def shards(queries, keys, values, out_grad, out_weight, send_slot, recv_index, packed_doc):
     row = lambda a: a.reshape(1, TOK)
-    col = lambda a: a.reshape(TOK, 1)
     vmem = pl.BlockSpec(memory_space=pltpu.VMEM)
+    hbm = pl.BlockSpec(memory_space=pl.ANY)
     dma = pltpu.SemaphoreType.DMA
-    return pl.pallas_call(
+    grads = pl.pallas_call(
         kernel,
         out_shape=(
             jax.ShapeDtypeStruct((TOK, NB * BLK), BF),
@@ -340,9 +361,14 @@
             jax.ShapeDtypeStruct((TOK, HEAD_DIM), BF),
             jax.ShapeDtypeStruct((ROWS, NB * BLK), F32),
         ),
-        in_specs=[vmem] * 11,
+        in_specs=[hbm, hbm, hbm, vmem, hbm, vmem, vmem, vmem],
         out_specs=(vmem,) * 4,
         scratch_shapes=[
+            pltpu.VMEM((TOK, NB * BLK), BF),
+            pltpu.VMEM((TOK, HEAD_DIM), BF),
+            pltpu.VMEM((TOK, HEAD_DIM), BF),
+            pltpu.VMEM((NB * BLK, FEAT), BF),
+            dma((4,)),
             pltpu.VMEM((LANES, PART), BF),
             pltpu.VMEM((LANES, PART), BF),
             pltpu.VMEM((NB + 1, LANES, BLK), BF),
@@ -379,9 +405,15 @@
         name="packed_attention_backward",
     )(
         queries, keys, values, out_grad, out_weight,
-        row(send_slot), col(send_slot), row(recv_index), col(recv_index),
-        row(packed_doc), col(packed_doc),
+        row(send_slot), row(recv_index), row(packed_doc),
     )
+    return pl.pallas_call(
+        hand_on,
+        out_shape=tuple(jax.ShapeDtypeStruct(a.shape, a.dtype) for a in grads),
+        in_specs=[vmem] * 4,
+        out_specs=(vmem,) * 4,
+        name="results",
+    )(*grads)
 
 
 def solution(mesh):

time: 196 us -> 179 us (0.913)
  local copies, waits for them, and re-layouts: 11.8 us -> 0 us
  Pallas kernels: 184 us -> 178 us
    pallas_call x1, Pallas kernels: 184 us -> 175 us  [shards(): pl.pallas_call(kernel, out_shape=(jax.ShapeDtypeStruct((TOK, NB * BLK), B...]
    unnamed x4 -> x0, local copies, waits for them, and re-layouts: 7.16 us -> none
    reshape x3 -> x0, local copies, waits for them, and re-layouts: 4.6 us -> none  [shards(): col = lambda a: a.reshape(TOK, 1)]
    pallas_call x0 -> x1, Pallas kernels: none -> 2.64 us  [shards(): pl.pallas_call(hand_on, out_shape=tuple((jax.ShapeDtypeStruct(a.shape, a....]
where the time goes in v3:
time: 179 us; the launch traced here: 178 us
  Pallas kernels  178 us (99%)
    pallas_call x1, Pallas kernels, shards(): pl.pallas_call(kernel, out_shape=(jax.ShapeDtypeStruct((TOK, NB * BLK), B...  175 us

profile of v3, /device:TPU:4, one launch (start us, length us, event | category | flops | bytes accessed | tf_op | source)
XLA Modules:
  0.0 178.3 jit_solution(15134765287367612308)
XLA Ops:
  0.6 175.0 %packed_attention_backward.1 = (bf16[512,1024]{1,0:T(8,128)(2,1)}, bf16[512,128]{1,0:T(8,128)(2,1)}, bf16[512,128]{1,0:T(8,128)(2,1)}, f32[96,1024]{1,0:T(8,128)}) custom-call(bf16[512,1024]{1,0:T(8,128)(2,1)} %q_hbm.1, bf16[512,128]{1,0:T(8,128)(2,1)} %k_hbm.1, bf16[512,128]{1,0:T(8,128)(2,1)} %v_hbm.1, bf16[512,384]{1,0:T(8,128)(2,1)} %g_ref.1, ...), custom_call_target="tpu_custom_call" | custom-call | tf_op jit(solution)/shard_map/packed_attention_backward/pallas_call | solution.py:356
  175.7 2.6 %results.1 = (bf16[512,1024]{1,0:T(8,128)(2,1)}, bf16[512,128]{1,0:T(8,128)(2,1)}, bf16[512,128]{1,0:T(8,128)(2,1)}, f32[96,1024]{1,0:T(8,128)}) custom-call(bf16[512,1024]{1,0:T(8,128)(2,1)} %get-tuple-element.8.refs_0_, bf16[512,128]{1,0:T(8,128)(2,1)} %get-tuple-element.9.refs_1_, bf16[512,128]{1,0:T(8,128)(2,1)} %get-tuple-element.10.refs_2_, ...), custom_call_target="tpu_custom_call" | custom-call | tf_op jit(solution)/shard_map/results/pallas_call | solution.py:410

commit v4 on v3

--- a/solution.py
+++ b/solution.py
@@ -25,6 +25,7 @@
 FEAT = 3072
 ROWS = FEAT // NDP
 SLAB = NZ * ROWS
+HALF = TOK // 2
 
 
 def nn(a, b):
@@ -44,9 +45,10 @@
     qg_ref, kg_ref, vg_ref, wg_ref,
     q_ref, k_ref, v_ref, w_ref, sem_in,
     send_g, recv_g, send_x, recv_x, back, home,
-    sel_r, sel_rt, gt, bias, kv, kvt, dkv, hgt, att, dqt,
-    part, ya, yb, yc, yt, za, zb,
+    sel_r, sel_rt, gt, bias, kv, kvt, dkv, hgt, dqt,
+    weights, g4, att4, yt, za, zb,
     sem_gs, sem_gr, sem_xs, sem_xr, sem_bs, sem_br, sem_as, sem_ar, sem_ys, sem_yr, sem_zs, sem_zr,
+    sem_4s, sem_4r,
 ):
     me = lax.axis_index("dp")
     tp = lax.axis_index("tensor")
@@ -89,7 +91,7 @@
     def rows_of(d):
         return pl.ds(pl.multiple_of(d * CAP, CAP), CAP)
 
-    def exchange(src, dst, s_sem, r_sem):
+    def exchange(src, dst, s_sem, r_sem, lo=1, hi=NDP):
         def one(k, _):
             d = peer(k)
             pltpu.make_async_remote_copy(
@@ -98,8 +100,9 @@
             ).start()
             return 0
 
-        lax.fori_loop(1, NDP, one, 0)
-        dst[rows_of(me)] = src[rows_of(me)]
+        lax.fori_loop(lo, hi, one, 0)
+        if lo == 1:
+            dst[rows_of(me)] = src[rows_of(me)]
 
     def drain(ref, sem):
         whole = ref.at[pl.ds(0, LANES - CAP)]
@@ -183,39 +186,37 @@
     loads[3].wait()
     inv = 1.0 / math.sqrt(HEAD_DIM)
     norm = 1.0 / math.sqrt(TOK * NDP)
-    HALF = TOK // 2
 
     def head_block(j):
         rows = pl.ds(pl.multiple_of(j * BLK, BLK), BLK)
+        qp = nn(sel_r[...], recv_x[j]).astype(BF)
+        places = [(h, b) for h in range(2) for b in range(2)]
+
+        def cut(h, b):
+            kn = HALF * (b + 1)
+            return kn, slice(h * HEAD_DIM, (h + 1) * HEAD_DIM), slice(b * HALF, (b + 1) * HALF)
+
+        for h, b in places:
+            kn, hs, ps = cut(h, b)
+            s = nt(kv[:kn, :HEAD_DIM], qp[ps, hs]) + bias[:kn, ps]
+            top = jnp.max(s, axis=0, keepdims=True)
+            e = jnp.exp((s - top) * inv)
+            soft = e * (1.0 / jnp.sum(e, axis=0, keepdims=True))
+            weights[h, b, :kn] = soft
+            att4[j, my_y, hs, ps] = nn(kvt[HEAD_DIM:, :kn], soft.astype(BF)).astype(BF)
+
+        a_start(j)
         hgt[...] = nn(w_ref[rows, :], gt[...]).astype(BF)
-        qp = nn(sel_r[...], recv_x[j]).astype(BF)
-        for h in range(2):
-            hs = slice(h * HEAD_DIM, (h + 1) * HEAD_DIM)
-            for b in range(2):
-                kn = HALF * (b + 1)
-                ps = slice(b * HALF, (b + 1) * HALF)
-                qh = qp[ps, hs]
-                keys, vals = kv[:kn, :HEAD_DIM], kv[:kn, HEAD_DIM:]
-                s = nt(keys, qh) + bias[:kn, ps]
-                top = jnp.max(s, axis=0, keepdims=True)
-                e = jnp.exp((s - top) * inv)
-                soft = e * (1.0 / jnp.sum(e, axis=0, keepdims=True))
-                soft_half = soft.astype(BF)
-                att[hs, ps] = nn(kvt[HEAD_DIM:, :kn], soft_half).astype(BF)
-                hg = hgt[hs, ps]
-                dp_ = nn(vals, hg)
-                inner = jnp.sum(soft * dp_, axis=0, keepdims=True)
-                ds = (soft * (dp_ - inner)).astype(BF)
-                dqt[hs, ps] = (nn(kvt[:HEAD_DIM, :kn], ds) * inv).astype(BF)
-                dkv[:kn, :HEAD_DIM] += nn(ds, qh)
-                dkv[:kn, HEAD_DIM:] += nt(soft_half, hg)
-
-        def weight_slab(y, _):
-            rows = pl.ds(pl.multiple_of(y * SLAB, SLAB), SLAB)
-            part[j, y] = (nt(gt[rows, :], att[...]) * norm).astype(BF).reshape(NZ, ROWS, BLK)
-            return 0
-
-        lax.fori_loop(0, NY, weight_slab, 0)
+        for h, b in places:
+            kn, hs, ps = cut(h, b)
+            soft = weights[h, b, :kn]
+            hg = hgt[hs, ps]
+            dp_ = nn(kv[:kn, HEAD_DIM:], hg)
+            inner = jnp.sum(soft * dp_, axis=0, keepdims=True)
+            ds = (soft * (dp_ - inner)).astype(BF)
+            dqt[hs, ps] = (nn(kvt[:HEAD_DIM, :kn], ds) * inv).astype(BF)
+            dkv[:kn, :HEAD_DIM] += nn(ds, qp[ps, hs])
+            dkv[:kn, HEAD_DIM:] += nt(soft.astype(BF), hg)
 
     def yid(k):
         return lax.rem(my_y + k + 2 * NY, NY)
@@ -235,24 +236,90 @@
     def sgn(j):
         return 1 - 2 * lax.rem(j, 2)
 
-    def y_start(j):
+    def a_start(j):
+        mine_ = att4.at[j, my_y]
+        send(mine_, mine_, sem_ys.at[j, 0], sem_yr.at[j, 0], dp_dev(1, 0))
+        send(mine_, mine_, sem_ys.at[j, 1], sem_yr.at[j, 1], dp_dev(-1, 0))
+
+    low, high = pl.ds(0, BLK // 2), pl.ds(BLK // 2, BLK // 2)
+
+    def a_next(j):
+        below, above = att4.at[j, yid(-1)], att4.at[j, yid(1)]
+        landed(below, sem_yr.at[j, 0])
+        send(below.at[low], below.at[low], sem_ys.at[j, 2], sem_yr.at[j, 2], dp_dev(1, 0))
+        landed(above, sem_yr.at[j, 1])
+        send(above.at[high], above.at[high], sem_ys.at[j, 3], sem_yr.at[j, 3], dp_dev(-1, 0))
+
+    def a_end(j):
         g = sgn(j)
-        send(part.at[j, yid(2 * g)], ya.at[j], sem_ys.at[j, 0], sem_yr.at[j, 0], dp_dev(g, 0))
-        send(part.at[j, yid(-g)], yb.at[j], sem_ys.at[j, 1], sem_yr.at[j, 1], dp_dev(-g, 0))
-
-    def y_next(j):
-        g = sgn(j)
-        landed(ya.at[j], sem_yr.at[j, 0])
-        ya[j] = (ya[j].astype(F32) + part[j, yid(g)].astype(F32)).astype(BF)
-        send(ya.at[j], yc.at[j], sem_ys.at[j, 2], sem_yr.at[j, 2], dp_dev(g, 0))
-
-    def y_end(j):
-        g = sgn(j)
-        landed(yb.at[j], sem_yr.at[j, 1])
-        landed(yc.at[j], sem_yr.at[j, 2])
-        yt[j] = (yb[j].astype(F32) + yc[j].astype(F32) + part[j, my_y].astype(F32)).astype(BF)
+        opposite = att4.at[j, yid(2)]
+        landed(opposite.at[low], sem_yr.at[j, 2])
+        landed(opposite.at[high], sem_yr.at[j, 3])
+
+        def slab(i, _):
+            rows = pl.ds(pl.multiple_of(i * 2 * ROWS, 2 * ROWS), 2 * ROWS)
+            tot = nt(g4[0, rows, :], att4[j, 0])
+            for y in range(1, NY):
+                tot += nt(g4[y, rows, :], att4[j, y])
+            yt[j, pl.ds(2 * i, 2)] = (tot * norm).astype(BF).reshape(2, ROWS, BLK)
+            return 0
+
+        lax.fori_loop(0, NZ // 2, slab, 0)
         send(yt.at[j, zid(4 * g)], za.at[j, 0], sem_zs.at[j, 0], sem_zr.at[j, 0], dp_dev(0, g))
         send(yt.at[j, zid(-3 * g)], zb.at[j, 0], sem_zs.at[j, 4], sem_zr.at[j, 4], dp_dev(0, -g))
+
+    def mine4(t, lo=0, n=ROWS):
+        return pl.ds(pl.multiple_of(t * ROWS + lo, 16), n)
+
+    def chunk(y):
+        return gt.at[pl.ds(pl.multiple_of(y * SLAB + tp * ROWS, 16), ROWS)]
+
+    def g4_start():
+        for k in range(1, NY):
+            y = lax.rem(my_y + k, NY)
+            send(chunk(y), g4.at[my_y, mine4(tp)], sem_4s.at[8], sem_4r.at[8], y * NZ + my_z)
+        g4[my_y, mine4(tp)] = chunk(my_y)[...]
+
+    def three(sem):
+        ref = g4.at[pl.ds(0, NY - 1), pl.ds(0, ROWS)]
+        pltpu.make_async_copy(ref, ref, sem).wait()
+
+    def ring4(idx, t, lo, n, dev):
+        ref = g4.at[:, mine4(t, lo, n)]
+        pltpu.make_async_remote_copy(
+            src_ref=ref, dst_ref=ref, send_sem=sem_4s.at[idx], recv_sem=sem_4r.at[idx],
+            device_id={"tensor": dev}, device_id_type=MESH,
+        ).start()
+
+    def got4(idx, t, lo, n):
+        landed(g4.at[:, mine4(t, lo, n)], sem_4r.at[idx])
+
+    hop = ROWS // 2
+
+    def g4_one():
+        three(sem_4r.at[8])
+        ring4(0, tp, 0, ROWS, right)
+        ring4(1, tp, 0, ROWS, left)
+        ring4(2, tp, 0, ROWS, twin)
+
+    def g4_two():
+        got4(0, left, 0, ROWS)
+        ring4(3, left, 0, hop, right)
+        ring4(4, left, 0, ROWS, twin)
+        got4(1, right, 0, ROWS)
+        ring4(5, right, hop, hop, left)
+        ring4(6, right, 0, ROWS, twin)
+
+    def g4_three():
+        got4(3, far, 0, hop)
+        got4(5, far, hop, hop)
+        ring4(7, far, 0, ROWS, twin)
+
+    def g4_four():
+        got4(2, x_dev(0, 1 - core), 0, ROWS)
+        got4(4, x_dev(-1, 1 - core), 0, ROWS)
+        got4(6, x_dev(1, 1 - core), 0, ROWS)
+        got4(7, x_dev(2, 1 - core), 0, ROWS)
 
     def z_next(j, s):
         g = sgn(j)
@@ -269,47 +336,62 @@
             cols = pl.ds(pl.multiple_of(j * BLK, BLK), BLK)
             wg_ref[:, cols] = za[j, 3].astype(F32) + zb[j, 2].astype(F32) + yt[j, my_z].astype(F32)
 
+    def push_back(j, lo=1, hi=NDP):
+        exchange(back.at[j], home.at[j], sem_bs.at[j], sem_br.at[j], lo, hi)
+
     def step(j, _):
         drain(recv_x.at[j], sem_xr.at[j])
         head_block(j)
-        y_start(j)
         back[j] = nt(sel_rt[...], dqt[...]).astype(BF)
-        exchange(back.at[j], home.at[j], sem_bs.at[j], sem_br.at[j])
-
-        @pl.when(j >= 1)
+        @pl.when((j >= 1) & (j < 3))
         def _():
-            y_next(j - 1)
+            a_next(j - 1)
+
+        pl.when(j == 0)(g4_one)
+        pl.when(j == 1)(g4_two)
+        pl.when(j == 2)(g4_three)
+
+        @pl.when(j >= 2)
+        def _():
+            push_back(j - 2)
 
         return 0
 
+    g4_start()
     lax.fori_loop(0, NB, step, 0)
 
     lane = lax.broadcasted_iota(jnp.int32, (TOK, 2 * HEAD_DIM), 1)
     dkv_h = (dkv[...] * jnp.where(lane < HEAD_DIM, inv, 1.0)).astype(BF)
     back[NB] = nn(sel_rt[...], dkv_h).astype(BF)
-    exchange(back.at[NB], home.at[NB], sem_bs.at[NB], sem_br.at[NB])
 
     sel_r[...] = (slot_cols == column(ss_row)).astype(BF)
     def settle(j):
         drain(home.at[j], sem_br.at[j])
         return nn(sel_r[...], home[j]).astype(BF)
 
-    y_end(0)
-    y_end(1)
+    g4_four()
+    a_end(0)
+    a_next(2)
+    a_end(1)
+    push_back(2, 1, NDP // 2)
     z_next(0, 0)
-    y_next(3)
-    y_end(2)
     z_next(1, 0)
+    push_back(2, NDP // 2, NDP)
+    a_next(3)
     z_next(0, 1)
     z_next(1, 1)
+    a_end(2)
+    push_back(3, 1, NDP // 2)
+    z_next(0, 2)
+    z_next(1, 2)
     z_next(2, 0)
-    z_next(0, 2)
-    y_end(3)
-    z_next(1, 2)
+    a_end(3)
+    push_back(3, NDP // 2, NDP)
+    z_next(0, 3)
+    z_next(1, 3)
     z_next(2, 1)
-    z_next(0, 3)
     z_next(3, 0)
-    z_next(1, 3)
+    push_back(NB)
     z_next(2, 2)
     z_next(3, 1)
     z_next(2, 3)
@@ -333,14 +415,18 @@
         c.wait_send()
 
     def ring_sent(j, _):
-        landed(ya.at[j], sem_ys.at[j, 0])
-        landed(ya.at[j], sem_ys.at[j, 1])
-        landed(ya.at[j], sem_ys.at[j, 2])
+        landed(att4.at[j, 0], sem_ys.at[j, 0])
+        landed(att4.at[j, 0], sem_ys.at[j, 1])
+        landed(att4.at[j, 0].at[low], sem_ys.at[j, 2])
+        landed(att4.at[j, 0].at[low], sem_ys.at[j, 3])
         for s in range(7):
             landed(za.at[j, 0], sem_zs.at[j, s])
         return 0
 
     lax.fori_loop(0, NB, ring_sent, 0)
+    three(sem_4s.at[8])
+    for i in range(8):
+        landed(g4.at[:, mine4(0, 0, hop if i in (3, 5) else ROWS)], sem_4s.at[i])
 
 
 def hand_on(*refs):
@@ -384,11 +470,9 @@
             pltpu.VMEM((TOK, BLK), F32),
             pltpu.VMEM((BLK, TOK), BF),
             pltpu.VMEM((BLK, TOK), BF),
-            pltpu.VMEM((BLK, TOK), BF),
-            pltpu.VMEM((NB, NY, NZ, ROWS, BLK), BF),
-            pltpu.VMEM((NB, NZ, ROWS, BLK), BF),
-            pltpu.VMEM((NB, NZ, ROWS, BLK), BF),
-            pltpu.VMEM((NB, NZ, ROWS, BLK), BF),
+            pltpu.VMEM((2, 2, TOK, HALF), F32),
+            pltpu.VMEM((NY, SLAB, TOK), BF),
+            pltpu.VMEM((NB, NY, BLK, TOK), BF),
             pltpu.VMEM((NB, NZ, ROWS, BLK), BF),
             pltpu.VMEM((NB, 4, ROWS, BLK), BF),
             pltpu.VMEM((NB, 3, ROWS, BLK), BF),
@@ -396,8 +480,9 @@
             dma((NB + 1,)), dma((NB + 1,)),
             dma((NB + 1,)), dma((NB + 1,)),
             dma((8,)), dma((8,)),
-            dma((NB, 3)), dma((NB, 3)),
+            dma((NB, 4)), dma((NB, 4)),
             dma((NB, 7)), dma((NB, 7)),
+            dma((9,)), dma((9,)),
         ],
         compiler_params=pltpu.CompilerParams(
             collective_id=1, has_side_effects=True, vmem_limit_bytes=60 << 20

time: 179 us -> 168 us (0.939)
  Pallas kernels: 178 us -> 168 us
    pallas_call x1, Pallas kernels: 175 us -> 165 us  [shards(): pl.pallas_call(kernel, out_shape=(jax.ShapeDtypeStruct((TOK, NB * BLK), B...]
where the time goes in v4:
time: 168 us
  Pallas kernels  168 us (100%)
    pallas_call x1, Pallas kernels, shards(): pl.pallas_call(kernel, out_shape=(jax.ShapeDtypeStruct((TOK, NB * BLK), B...  165 us

profile of v4, /device:TPU:4, one launch (start us, length us, event | category | flops | bytes accessed | tf_op | source)
XLA Modules:
  0.0 168.2 jit_solution(8742229793432884383)
XLA Ops:
  0.6 165.0 %packed_attention_backward.1 = (bf16[512,1024]{1,0:T(8,128)(2,1)}, bf16[512,128]{1,0:T(8,128)(2,1)}, bf16[512,128]{1,0:T(8,128)(2,1)}, f32[96,1024]{1,0:T(8,128)}) custom-call(bf16[512,1024]{1,0:T(8,128)(2,1)} %q_hbm.1, bf16[512,128]{1,0:T(8,128)(2,1)} %k_hbm.1, bf16[512,128]{1,0:T(8,128)(2,1)} %v_hbm.1, bf16[512,384]{1,0:T(8,128)(2,1)} %g_ref.1, ...), custom_call_target="tpu_custom_call" | custom-call | tf_op jit(solution)/shard_map/packed_attention_backward/pallas_call | solution.py:442
  165.6 2.6 %results.1 = (bf16[512,1024]{1,0:T(8,128)(2,1)}, bf16[512,128]{1,0:T(8,128)(2,1)}, bf16[512,128]{1,0:T(8,128)(2,1)}, f32[96,1024]{1,0:T(8,128)}) custom-call(bf16[512,1024]{1,0:T(8,128)(2,1)} %get-tuple-element.8.refs_0_, bf16[512,128]{1,0:T(8,128)(2,1)} %get-tuple-element.9.refs_1_, bf16[512,128]{1,0:T(8,128)(2,1)} %get-tuple-element.10.refs_2_, ...), custom_call_target="tpu_custom_call" | custom-call | tf_op jit(solution)/shard_map/results/pallas_call | solution.py:495

commit v5 on v4

--- a/solution.py
+++ b/solution.py
@@ -390,14 +390,17 @@
     z_next(0, 3)
     z_next(1, 3)
     z_next(2, 1)
+    qg_ref[:, 0 * BLK:1 * BLK] = settle(0)
     z_next(3, 0)
+    z_next(2, 2)
+    qg_ref[:, 1 * BLK:2 * BLK] = settle(1)
+    z_next(3, 1)
     push_back(NB)
-    z_next(2, 2)
-    z_next(3, 1)
     z_next(2, 3)
+    qg_ref[:, 2 * BLK:3 * BLK] = settle(2)
     z_next(3, 2)
     z_next(3, 3)
-    for j in range(NB):
+    for j in range(3, NB):
         qg_ref[:, j * BLK:(j + 1) * BLK] = settle(j)
     got = settle(NB)
     kg_ref[...] = got[:, :HEAD_DIM]

time: 168 us -> 166 us (0.988)
  Pallas kernels: 168 us -> 166 us
    pallas_call x1, Pallas kernels: 165 us -> 163 us  [shards(): pl.pallas_call(kernel, out_shape=(jax.ShapeDtypeStruct((TOK, NB * BLK), B...]
where the time goes in v5:
time: 166 us
  Pallas kernels  166 us (100%)
    pallas_call x1, Pallas kernels, shards(): pl.pallas_call(kernel, out_shape=(jax.ShapeDtypeStruct((TOK, NB * BLK), B...  163 us

profile of v5, /device:TPU:4, one launch (start us, length us, event | category | flops | bytes accessed | tf_op | source)
XLA Modules:
  0.0 166.2 jit_solution(3952752625099489332)
XLA Ops:
  0.6 162.9 %packed_attention_backward.1 = (bf16[512,1024]{1,0:T(8,128)(2,1)}, bf16[512,128]{1,0:T(8,128)(2,1)}, bf16[512,128]{1,0:T(8,128)(2,1)}, f32[96,1024]{1,0:T(8,128)}) custom-call(bf16[512,1024]{1,0:T(8,128)(2,1)} %q_hbm.1, bf16[512,128]{1,0:T(8,128)(2,1)} %k_hbm.1, bf16[512,128]{1,0:T(8,128)(2,1)} %v_hbm.1, bf16[512,384]{1,0:T(8,128)(2,1)} %g_ref.1, ...), custom_call_target="tpu_custom_call" | custom-call | tf_op jit(solution)/shard_map/packed_attention_backward/pallas_call | solution.py:445
  163.6 2.6 %results.1 = (bf16[512,1024]{1,0:T(8,128)(2,1)}, bf16[512,128]{1,0:T(8,128)(2,1)}, bf16[512,128]{1,0:T(8,128)(2,1)}, f32[96,1024]{1,0:T(8,128)}) custom-call(bf16[512,1024]{1,0:T(8,128)(2,1)} %get-tuple-element.8.refs_0_, bf16[512,128]{1,0:T(8,128)(2,1)} %get-tuple-element.9.refs_1_, bf16[512,128]{1,0:T(8,128)(2,1)} %get-tuple-element.10.refs_2_, ...), custom_call_target="tpu_custom_call" | custom-call | tf_op jit(solution)/shard_map/results/pallas_call | solution.py:498
